TPU v7x, 32 devices: a whole 2x2x4 slice. The times are simulated.
32 devices in a mesh: dp: 8 (over y, x, core), mp: 4 (over z).
Axes of the slice: x: 2, y: 2, z: 4, core: 2. Of those that a mesh axis runs over, the one named last changes fastest.
Arguments:
- tokens: bfloat16 [512, 40, 768], P(('dp', 'mp')), may hold values from -6 to 6
- patches: bfloat16 [128, 145, 1024], P('dp'), may hold values from -6 to 6
- image_rows: int32 [8, 16], P('dp'), may hold values from 1 to 7, 64 in all within a row
- row_lengths: int32 [512], P('dp'), may hold values from 4 to 40, as said below
- box_mask: int32 [512, 145], P('dp'), may hold values from 0 to 1, as said below
- self_project: bfloat16 [3, 768, 768], P(None, None, 'mp'), may hold values from -0.21875 to 0.21875
- self_output: bfloat16 [768, 768], P('mp'), may hold values from -0.875 to 0.875
- first_gain: float32 [768], replicated, may hold values from 0.5 to 1.5
- first_shift: float32 [768], replicated, may hold values from -2 to 2
- cross_query: bfloat16 [768, 768], P(None, 'mp'), may hold values from -0.21875 to 0.21875
- cross_keyval: bfloat16 [2, 1024, 768], P(None, None, 'mp'), may hold values from -0.1875 to 0.1875
- cross_output: bfloat16 [768, 768], P('mp'), may hold values from -0.875 to 0.875
- second_gain: float32 [768], replicated, may hold values from 0.5 to 1.5
- second_shift: float32 [768], replicated, may hold values from -2 to 2
- expand_weight: bfloat16 [768, 3072], P(None, 'mp'), may hold values from -0.21875 to 0.21875
- expand_bias: float32 [3072], P('mp'), may hold values from -3 to 3
- shrink_weight: bfloat16 [3072, 768], P('mp'), may hold values from -0.109375 to 0.109375
- third_gain: float32 [768], replicated, may hold values from 0.5 to 1.5
- third_shift: float32 [768], replicated, may hold values from -2 to 2
- cotangent: bfloat16 [512, 40, 768], P(('dp', 'mp')), may hold values from -6 to 6
Outputs:
- joined_text: bfloat16 [512, 40, 768], P(('dp', 'mp'))
- text_grad: float32 [512, 40, 768], P(('dp', 'mp'))
- patch_grad: float32 [128, 145, 1024], P('dp', None, 'mp')
- self_project_grad: float32 [3, 768, 768], P(None, None, 'mp')
- self_output_grad: float32 [768, 768], P('mp')
- first_gain_grad: float32 [768], replicated
- first_shift_grad: float32 [768], replicated
- cross_query_grad: float32 [768, 768], P(None, 'mp')
- cross_keyval_grad: float32 [2, 1024, 768], P(None, None, 'mp')
- cross_output_grad: float32 [768, 768], P('mp')
- second_gain_grad: float32 [768], replicated
- second_shift_grad: float32 [768], replicated
- expand_weight_grad: float32 [768, 3072], P(None, 'mp')
- expand_bias_grad: float32 [3072], P('mp')
- shrink_weight_grad: float32 [3072, 768], P('mp')
- third_gain_grad: float32 [768], replicated
- third_shift_grad: float32 [768], replicated
Inputs may be any that keep to these rules, and one draw needn't show every extreme that they name: `image_rows`: rows of each image, in the order of the 64 rows of its index of dp; each index's counts sum to 64. An image's first row is its caption, the others are its box phrases. `row_lengths`: tokens in use at the start of each row; every row whose number is a multiple of 16 uses all 40. `box_mask`: 1 at patch 0 and at the patches 1 + 12 * i + j of a rectangle of 3 or more by 3 or more cells of the 12 by 12 grid; read only for rows that are not captions.
All inputs are finite; a program needn't handle non-finite values.
Results may differ from a plain program's by a relative error of at most 0.02.
Values may be sent and summed in bfloat16 or wider, within the bound.
A program may use at most 256 MiB of HBM per device.

v0:
```python
import jax
import jax.numpy as jnp
from jax import lax
from jax.sharding import PartitionSpec as P

HEAD_DIM = 64


highest = lax.Precision.HIGHEST


def rows_structure(counts, group_rows):
    row_ends = jnp.cumsum(counts)
    starts = row_ends - counts
    row_index = jnp.arange(group_rows, dtype=jnp.int32)[:, None]
    member = (row_index >= starts[None, :]) & (row_index < row_ends[None, :])
    caption = jnp.any(row_index == starts[None, :], axis=1)
    return (member, caption)


def normalize(hidden):
    center = hidden - jnp.mean(hidden, axis=-1, keepdims=True)
    inverse = lax.rsqrt(jnp.mean(center * center, axis=-1, keepdims=True) + 1e-06)
    return (center * inverse, inverse)


def norm_back(upstream, scaled, inverse, norm_gain):
    scaled_grad = upstream * norm_gain
    return inverse * (
        scaled_grad
        - jnp.mean(scaled_grad, axis=-1, keepdims=True)
        - scaled * jnp.mean(scaled_grad * scaled, axis=-1, keepdims=True)
    )


def split_heads(values):
    return values.reshape(values.shape[0], values.shape[1], values.shape[2] // HEAD_DIM, HEAD_DIM)


def masked_scores(queries, key_rows, allowed):
    scores = jnp.einsum(
        "gqhe,gkhe->ghqk",
        split_heads(queries),
        split_heads(key_rows),
        preferred_element_type=jnp.float32,
    ) * HEAD_DIM ** (-0.5)
    return jnp.where(allowed[:, None, None, :], scores, -1000000000.0)


def attend(queries, key_rows, value_rows, allowed):
    scores = masked_scores(queries, key_rows, allowed)
    row_peak = jnp.max(scores, axis=-1, keepdims=True)
    raised = jnp.exp(scores - row_peak)
    row_total = jnp.sum(raised, axis=-1, keepdims=True)
    weights = (raised / row_total).astype(jnp.bfloat16)
    context = jnp.einsum(
        "ghqk,gkhe->gqhe", weights, split_heads(value_rows), preferred_element_type=jnp.float32
    )
    return (context.reshape(queries.shape), row_peak + jnp.log(row_total))


def attend_back(queries, key_rows, value_rows, allowed, row_lse, context_grad):
    scores = masked_scores(queries, key_rows, allowed)
    probs = jnp.exp(scores - row_lse)
    weights = probs.astype(jnp.bfloat16)
    grad_heads = split_heads(context_grad)
    prob_grad = jnp.einsum(
        "gqhe,gkhe->ghqk", grad_heads, split_heads(value_rows), preferred_element_type=jnp.float32
    )
    score_low = (probs * (prob_grad - jnp.sum(probs * prob_grad, axis=-1, keepdims=True))).astype(
        jnp.bfloat16
    )
    query_grad = jnp.einsum(
        "ghqk,gkhe->gqhe", score_low, split_heads(key_rows), preferred_element_type=jnp.float32
    ) * HEAD_DIM ** (-0.5)
    key_grad = jnp.einsum(
        "ghqk,gqhe->gkhe", score_low, split_heads(queries), preferred_element_type=jnp.float32
    ) * HEAD_DIM ** (-0.5)
    value_grad = jnp.einsum(
        "ghqk,gqhe->gkhe", weights, grad_heads, preferred_element_type=jnp.float32
    )
    return (
        query_grad.reshape(queries.shape),
        key_grad.reshape(key_rows.shape),
        value_grad.reshape(value_rows.shape),
    )


def gather_rows(local_rows):
    return lax.all_gather(local_rows, "mp", axis=0, tiled=True)


def gather_grads(local_grads):
    return lax.all_gather(local_grads, "mp", axis=0, tiled=True)


def scatter_out(inputs_all, weight):
    return lax.psum_scatter(
        jnp.dot(inputs_all, weight, preferred_element_type=jnp.float32),
        "mp",
        scatter_dimension=0,
        tiled=True,
    )


def back_term(pairs):
    terms = [
        lax.dot_general(
            grad_block, weight, (((2,), (1,)), ((), ())), preferred_element_type=jnp.float32
        )
        for grad_block, weight in pairs
    ]
    return sum(terms[1:], terms[0])


def scatter_back(pairs):
    return lax.psum_scatter(
        back_term(pairs).astype(jnp.bfloat16), "mp", scatter_dimension=0, tiled=True
    ).astype(jnp.float32)


def per_device(
    tokens,
    patches,
    image_rows,
    row_lengths,
    box_mask,
    self_project,
    self_output,
    first_gain,
    first_shift,
    cross_query,
    cross_keyval,
    cross_output,
    second_gain,
    second_shift,
    expand_weight,
    expand_bias,
    shrink_weight,
    third_gain,
    third_shift,
    cotangent,
):
    group_rows = row_lengths.shape[0]
    seq_slots = tokens.shape[1]
    member, caption = rows_structure(image_rows[0], group_rows)
    member_low = member.astype(jnp.bfloat16)
    member_full = member.astype(jnp.float32)
    key_ok = jnp.arange(seq_slots, dtype=jnp.int32)[None, :] < row_lengths[:, None]
    cross_ok = caption[:, None] | (box_mask > 0)
    text_all = gather_rows(tokens)
    queries = jnp.dot(text_all, self_project[0], preferred_element_type=jnp.float32).astype(
        jnp.bfloat16
    )
    key_rows = jnp.dot(text_all, self_project[1], preferred_element_type=jnp.float32).astype(
        jnp.bfloat16
    )
    value_rows = jnp.dot(text_all, self_project[2], preferred_element_type=jnp.float32).astype(
        jnp.bfloat16
    )
    self_context, self_lse = attend(queries, key_rows, value_rows, key_ok)
    self_low = self_context.astype(jnp.bfloat16)
    after_self = tokens.astype(jnp.float32) + scatter_out(self_low, self_output)
    first_scaled, first_inverse = normalize(after_self)
    first_value = first_scaled * first_gain + first_shift
    first_all = gather_rows(first_value.astype(jnp.bfloat16))
    cross_queries = jnp.dot(first_all, cross_query, preferred_element_type=jnp.float32).astype(
        jnp.bfloat16
    )
    image_keys = jnp.dot(patches, cross_keyval[0], preferred_element_type=jnp.float32).astype(
        jnp.bfloat16
    )
    image_values = jnp.dot(patches, cross_keyval[1], preferred_element_type=jnp.float32).astype(
        jnp.bfloat16
    )
    row_keys = jnp.einsum(
        "gi,ipe->gpe", member_low, image_keys, preferred_element_type=jnp.float32
    ).astype(jnp.bfloat16)
    row_values = jnp.einsum(
        "gi,ipe->gpe", member_low, image_values, preferred_element_type=jnp.float32
    ).astype(jnp.bfloat16)
    cross_context, cross_lse = attend(cross_queries, row_keys, row_values, cross_ok)
    cross_low = cross_context.astype(jnp.bfloat16)
    after_cross = first_value + scatter_out(cross_low, cross_output)
    second_scaled, second_inverse = normalize(after_cross)
    second_value = second_scaled * second_gain + second_shift
    second_low = second_value.astype(jnp.bfloat16)
    second_all = lax.all_gather(second_low, "mp", axis=0, tiled=True)
    expanded = jnp.dot(second_all, expand_weight, preferred_element_type=jnp.float32) + expand_bias
    activated = jax.nn.gelu(expanded, approximate=False).astype(jnp.bfloat16)
    after_feed = second_value + lax.psum_scatter(
        jnp.dot(activated, shrink_weight, preferred_element_type=jnp.float32),
        "mp",
        scatter_dimension=0,
        tiled=True,
    )
    third_scaled, third_inverse = normalize(after_feed)
    joined = (third_scaled * third_gain + third_shift).astype(jnp.bfloat16)
    upstream = cotangent.astype(jnp.float32)
    third_gain_grad = jnp.sum(upstream * third_scaled, axis=(0, 1))
    third_shift_grad = jnp.sum(upstream, axis=(0, 1))
    feed_grad = norm_back(upstream, third_scaled, third_inverse, third_gain)
    feed_low = feed_grad.astype(jnp.bfloat16)
    gelu_back = jax.vjp(lambda inner: jax.nn.gelu(inner, approximate=False), expanded)[1]
    feed_all = lax.all_gather(feed_low, "mp", axis=0, tiled=True)
    shrink_grad = jnp.einsum("glf,gld->fd", activated, feed_all, preferred_element_type=jnp.float32)
    activated_grad = jnp.einsum(
        "gld,fd->glf", feed_all, shrink_weight, preferred_element_type=jnp.float32
    )
    expand_low = gelu_back(activated_grad)[0].astype(jnp.bfloat16)
    expand_bias_grad = jnp.sum(expand_low.astype(jnp.float32), axis=(0, 1))
    expand_grad = jnp.einsum(
        "gld,glf->df", second_all, expand_low, preferred_element_type=jnp.float32
    )
    second_up = feed_grad + lax.psum_scatter(
        back_term([(expand_low, expand_weight)]), "mp", scatter_dimension=0, tiled=True
    )
    second_gain_grad = jnp.sum(second_up * second_scaled, axis=(0, 1))
    second_shift_grad = jnp.sum(second_up, axis=(0, 1))
    cross_grad = norm_back(second_up, second_scaled, second_inverse, second_gain)
    cross_all = gather_grads(cross_grad.astype(jnp.bfloat16))
    cross_output_grad = jnp.einsum(
        "gle,gld->ed", cross_low, cross_all, preferred_element_type=jnp.float32
    )
    context_low = jnp.einsum(
        "gld,ed->gle", cross_all, cross_output, preferred_element_type=jnp.float32
    ).astype(jnp.bfloat16)
    cross_qpart, cross_kpart, cross_vpart = attend_back(
        cross_queries, row_keys, row_values, cross_ok, cross_lse, context_low
    )
    cross_query_low = cross_qpart.astype(jnp.bfloat16)
    image_key_low = jnp.einsum("gi,gpe->ipe", member_full, cross_kpart, precision=highest).astype(
        jnp.bfloat16
    )
    image_value_low = jnp.einsum("gi,gpe->ipe", member_full, cross_vpart, precision=highest).astype(
        jnp.bfloat16
    )
    cross_query_grad = jnp.einsum(
        "gld,gle->de", first_all, cross_query_low, preferred_element_type=jnp.float32
    )
    cross_keyval_grad = jnp.stack(
        [
            jnp.einsum("ipc,ipe->ce", patches, image_key_low, preferred_element_type=jnp.float32),
            jnp.einsum("ipc,ipe->ce", patches, image_value_low, preferred_element_type=jnp.float32),
        ]
    )
    patch_term = jnp.einsum(
        "ipe,ce->ipc", image_key_low, cross_keyval[0], preferred_element_type=jnp.float32
    ) + jnp.einsum(
        "ipe,ce->ipc", image_value_low, cross_keyval[1], preferred_element_type=jnp.float32
    )
    patch_grad = lax.psum_scatter(
        patch_term.astype(jnp.bfloat16), "mp", scatter_dimension=2, tiled=True
    ).astype(jnp.float32)
    first_up = cross_grad + scatter_back([(cross_query_low, cross_query)])
    first_gain_grad = jnp.sum(first_up * first_scaled, axis=(0, 1))
    first_shift_grad = jnp.sum(first_up, axis=(0, 1))
    self_grad = norm_back(first_up, first_scaled, first_inverse, first_gain)
    self_all = gather_grads(self_grad.astype(jnp.bfloat16))
    self_output_grad = jnp.einsum(
        "gle,gld->ed", self_low, self_all, preferred_element_type=jnp.float32
    )
    self_context_low = jnp.einsum(
        "gld,ed->gle", self_all, self_output, preferred_element_type=jnp.float32
    ).astype(jnp.bfloat16)
    self_qpart, self_kpart, self_vpart = attend_back(
        queries, key_rows, value_rows, key_ok, self_lse, self_context_low
    )
    query_low = self_qpart.astype(jnp.bfloat16)
    key_low = self_kpart.astype(jnp.bfloat16)
    value_low = self_vpart.astype(jnp.bfloat16)
    self_project_grad = jnp.stack(
        [
            jnp.einsum("gld,gle->de", text_all, query_low, preferred_element_type=jnp.float32),
            jnp.einsum("gld,gle->de", text_all, key_low, preferred_element_type=jnp.float32),
            jnp.einsum("gld,gle->de", text_all, value_low, preferred_element_type=jnp.float32),
        ]
    )
    text_grad = self_grad + scatter_back(
        [(query_low, self_project[0]), (key_low, self_project[1]), (value_low, self_project[2])]
    )
    (
        self_project_grad,
        self_output_grad,
        cross_query_grad,
        cross_keyval_grad,
        cross_output_grad,
        expand_grad,
        expand_bias_grad,
        shrink_grad,
    ) = lax.psum(
        (
            self_project_grad,
            self_output_grad,
            cross_query_grad,
            cross_keyval_grad,
            cross_output_grad,
            expand_grad,
            expand_bias_grad,
            shrink_grad,
        ),
        "dp",
    )
    (
        first_gain_grad,
        first_shift_grad,
        second_gain_grad,
        second_shift_grad,
        third_gain_grad,
        third_shift_grad,
    ) = lax.psum(
        (
            first_gain_grad,
            first_shift_grad,
            second_gain_grad,
            second_shift_grad,
            third_gain_grad,
            third_shift_grad,
        ),
        ("dp", "mp"),
    )
    return (
        joined,
        text_grad,
        patch_grad,
        self_project_grad,
        self_output_grad,
        first_gain_grad,
        first_shift_grad,
        cross_query_grad,
        cross_keyval_grad,
        cross_output_grad,
        second_gain_grad,
        second_shift_grad,
        expand_grad,
        expand_bias_grad,
        shrink_grad,
        third_gain_grad,
        third_shift_grad,
    )


def solution(mesh):
    return jax.shard_map(
        per_device,
        mesh=mesh,
        in_specs=(
            P(("dp", "mp"), None, None),
            P("dp", None, None),
            P("dp", None),
            P("dp"),
            P("dp", None),
            P(None, None, "mp"),
            P("mp", None),
            P(),
            P(),
            P(None, "mp"),
            P(None, None, "mp"),
            P("mp", None),
            P(),
            P(),
            P(None, "mp"),
            P("mp"),
            P("mp", None),
            P(),
            P(),
            P(("dp", "mp"), None, None),
        ),
        out_specs=(
            P(("dp", "mp"), None, None),
            P(("dp", "mp"), None, None),
            P("dp", None, "mp"),
            P(None, None, "mp"),
            P("mp", None),
            P(),
            P(),
            P(None, "mp"),
            P(None, None, "mp"),
            P("mp", None),
            P(),
            P(),
            P(None, "mp"),
            P("mp"),
            P("mp", None),
            P(),
            P(),
        ),
        check_vma=False,
    )
```

profile of v0, /device:TPU:0, one launch (start us, length us, event | category | flops | bytes accessed | tf_op | source)
XLA Modules:
  0.0 1636.1 jit_solution(13626316468100488004)
XLA Ops:
  8.7 80.1 %all-gather.7.cloned.1.call-done = bf16[64,40,768]{2,1,0:T(8,128)(2,1)} async-done(((bf16[16,40,768]{2,1,0:T(8,128)(2,1)}), bf16[64,40,768]{2,1,0:T(8,128)(2,1)}) %all-gather.7.cloned.1.call-update) | async-done | bytes 3932176 | tf_op jit(solution)/shard_map/all_gather | solution.py:90
  98.0 5.1 convolution_convert_fusion.7
  103.2 4.1 copy.142
  107.3 4.1 copy.144
  111.4 4.4 convolution_convert_fusion.8
  115.8 4.1 copy.141
  119.9 4.1 copy.146
  138.7 5.6 fusion.90
  144.8 134.6 %reduce-scatter.8.cloned.1.call-done = f32[16,40,768]{2,1,0:T(8,128)} async-done(((f32[64,40,768]{2,1,0:T(8,128)}), f32[16,40,768]{2,1,0:T(8,128)}) %reduce-scatter.8.cloned.1.call-update) | async-done | bytes 1966096 | tf_op jit(solution)/shard_map/reduce_scatter | solution.py:98
  283.5 9.2 convolution_convert_fusion
  292.7 8.8 copy.153
  301.4 9.2 convolution_convert_fusion.1
  310.6 8.8 copy.151
  319.6 40.6 %all-gather.9.cloned.1.call-done = bf16[64,40,768]{2,1,0:T(8,128)(2,1)} async-done(((bf16[16,40,768]{2,1,0:T(8,128)(2,1)}), bf16[64,40,768]{2,1,0:T(8,128)(2,1)}) %all-gather.9.cloned.1.call-update) | async-done | bytes 3932176 | tf_op jit(solution)/shard_map/all_gather | solution.py:90
  360.3 4.4 convolution_convert_fusion.5
  364.7 4.1 copy.152
  368.8 4.1 copy.154
  372.9 5.3 fusion.17
  381.4 6.3 convert_bitcast_fusion.1
  387.7 4.2 copy.155
  391.9 4.6 copy.156
  396.5 5.6 fusion.85
  402.3 134.9 %reduce-scatter.10.cloned.1.call-done = f32[16,40,768]{2,1,0:T(8,128)} async-done(((f32[64,40,768]{2,1,0:T(8,128)}), f32[16,40,768]{2,1,0:T(8,128)}) %reduce-scatter.10.cloned.1.call-update) | async-done | bytes 1966096 | tf_op jit(solution)/shard_map/reduce_scatter | solution.py:98
  542.0 77.0 %all-gather.11.cloned.1.call-done = bf16[64,40,768]{2,1,0:T(8,128)(2,1)} async-done(((bf16[16,40,768]{2,1,0:T(8,128)(2,1)}), bf16[64,40,768]{2,1,0:T(8,128)(2,1)}) %all-gather.11.cloned.1.call-update) | async-done | bytes 3932176 | tf_op jit(solution)/shard_map/all_gather | solution.py:188
  619.0 22.8 %multiply_convert_fusion.1 = (bf16[64,40,768]{2,1,0:T(8,128)(2,1)S(1)}, f32[64,40,768]{2,1,0:T(8,128)}, f32[64,40,768]{2,1,0:T(8,128)}) fusion(f32[768]{0:T(1024)S(1)} %copy-done.76, bf16[64,40,768]{2,1,0:T(8,128)(2,1)} %all-gather.11.cloned.1.call-done, bf16[768,768]{1,0:T(8,128)(2,1)S(1)} %copy-done), kind=kOutput, calls=%fused_computation.9 | convolution fusion | flops 3149660160 | bytes 24775680 | tf_op jit(solution)/shard_map/dot_general | solution.py:189
  643.8 5.4 fusion.64
  649.2 134.9 %reduce-scatter.12.cloned.1.call-done = f32[16,40,768]{2,1,0:T(8,128)} async-done(((f32[64,40,768]{2,1,0:T(8,128)}), f32[16,40,768]{2,1,0:T(8,128)}) %reduce-scatter.12.cloned.1.call-update) | async-done | bytes 1966096 | tf_op jit(solution)/shard_map/reduce_scatter | solution.py:191
  790.0 77.0 %all-gather.13.cloned.1.call-done = bf16[64,40,768]{2,1,0:T(8,128)(2,1)} async-done(((bf16[16,40,768]{2,1,0:T(8,128)(2,1)}), bf16[64,40,768]{2,1,0:T(8,128)(2,1)}) %all-gather.13.cloned.1.call-update) | async-done | bytes 3932176 | tf_op jit(solution)/shard_map/all_gather | solution.py:205
  867.0 12.0 convert_reduce_fusion
  880.9 5.4 fusion.66
  886.4 134.9 %reduce-scatter.14.cloned.1.call-done = f32[16,40,768]{2,1,0:T(8,128)} async-done(((f32[64,40,768]{2,1,0:T(8,128)}), f32[16,40,768]{2,1,0:T(8,128)}) %reduce-scatter.14.cloned.1.call-update) | async-done | bytes 1966096 | tf_op jit(solution)/shard_map/reduce_scatter | solution.py:215
  1021.4 4.7 multiply_reduce_fusion.2
  1029.0 77.0 %all-gather.15.cloned.1.call-done = bf16[64,40,768]{2,1,0:T(8,128)(2,1)} async-done(((bf16[16,40,768]{2,1,0:T(8,128)(2,1)}), bf16[64,40,768]{2,1,0:T(8,128)(2,1)}) %all-gather.15.cloned.1.call-update) | async-done | bytes 3932176 | tf_op jit(solution)/shard_map/all_gather | solution.py:94
  1112.6 4.3 copy.158
  1117.0 7.8 multiply_reduce_fusion
  1124.8 5.8 multiply_convert_fusion
  1142.2 4.4 convolution_convert_fusion.2
  1146.6 71.4 %reduce-scatter.16.cloned.1.call-done = bf16[16,40,768]{2,1,0:T(8,128)(2,1)} async-done(((bf16[64,40,768]{2,1,0:T(8,128)(2,1)}), bf16[16,40,768]{2,1,0:T(8,128)(2,1)}) %reduce-scatter.16.cloned.1.call-update) | async-done | bytes 983056 | tf_op jit(solution)/shard_map/reduce_scatter | solution.py:117
  1224.3 11.5 fusion.8
  1235.8 13.0 copy.178
  1248.8 9.1 broadcast_multiply_fusion
  1257.9 12.8 copy.175
  1270.7 7.1 convolution_convert_fusion.9
  1282.7 4.0 add_convert_fusion
  1287.8 8.0 convolution_bitcast_fusion
  1295.9 5.4 all-gather.17.cloned.1.call-done
  1301.2 4.4 convolution_convert_fusion.3
  1305.6 4.5 copy.161
  1310.1 4.2 copy.162
  1314.3 5.1 convert_bitcast_fusion
  1319.5 4.2 copy.172
  1323.7 5.1 multiply_reduce_fusion.1
  1333.8 4.2 copy.166
  1338.0 4.6 fusion.44
  1342.5 4.1 copy.169
  1346.7 4.5 copy.170
  1351.1 4.5 copy.173
  1355.7 4.5 copy.167
  1367.6 8.1 convolution_bitcast_fusion.1
  1398.8 14.3 psum.108
  1413.2 42.8 %all-reduce = (f32[768]{0:T(1024)}, f32[768]{0:T(1024)}, f32[768]{0:T(1024)}, f32[768]{0:T(1024)}, f32[768]{0:T(1024)}, /*index=5*/f32[768]{0:T(1024)}) all-reduce(f32[768]{0:T(1024)S(1)} %get-tuple-element.70, f32[768]{0:T(1024)S(1)} %get-tuple-element.77, f32[768]{0:T(1024)S(1)} %copy-done.60, ...), channel_id=1, replica_groups=mesh['dp'=8,'mp'=4] {'dp','mp'}, use_global_device_ids=true, to_apply=%region_30.31 | all-reduce | flops 4608 | bytes 36864 | tf_op jit(solution)/shard_map/psum | solution.py:311
  1459.0 9.0 reduce-scatter.18.cloned.1.call-done
  1468.0 3.8 convert_add_fusion
  1471.8 147.1 %all-reduce.4.cloned.1.call-done = (f32[3,768,192]{1,2,0:T(8,128)}, f32[192,768]{1,0:T(8,128)}, f32[768,192]{0,1:T(8,128)}, f32[2,1024,192]{1,2,0:T(8,128)}, f32...) async-done(((f32[3,768,192]{1,2,0:T(8,128)}, f32[192,768]{1,0:T(8,128)}, f32[768,192]{0,1:T(8,128)}, f32[2,1024,192]{1,2,0:T(8,128)}, f32[192,768]{1,0:T(8,128)}, ...) | async-done | bytes 9830416 | tf_op jit(solution)/shard_map/psum | solution.py:291
  (269 shorter events, 129.9 us)
Async XLA Ops:
  7.2 611.9 %copy-start = (bf16[768,768]{1,0:T(8,128)(2,1)S(1)}, bf16[768,768]{1,0:T(8,128)(2,1)}, u32[]{:S(2)}) copy-start(bf16[768,768]{1,0:T(8,128)(2,1)} %param.34) | copy-start | bytes 3538948
  7.2 81.6 %all-gather.7.cloned.1.call-start = ((), (), s32[]{:S(2)}) async-start(), calls=%async_computation.7 | async-start | bytes 4915200 | tf_op jit(solution)/shard_map/all_gather | solution.py:90
  7.9 271.4 %reduce-scatter.8.cloned.1.call-start = ((), (), s32[]{:S(2)}) async-start(), calls=%async_computation.8 | async-start | bytes 9830400 | tf_op jit(solution)/shard_map/reduce_scatter | solution.py:98
  98.0 26.1 %copy-start.13 = (bf16[64,40,3,64]{3,1,2,0:T(8,128)(2,1)}, bf16[64,40,3,64]{3,1,2,0:T(8,128)(2,1)S(1)}, u32[]{:S(2)}) copy-start(bf16[64,40,3,64]{3,1,2,0:T(8,128)(2,1)S(1)} %copy.145) | copy-start | bytes 2949124
  126.8 3.0 copy-start.21
  135.4 8.9 copy-start.19
  135.4 3.3 copy-start.48
  144.4 137.4 %copy-start.54 = (f32[768]{0:T(1024)S(1)}, f32[768]{0:T(1024)}, u32[]{:S(2)}) copy-start(f32[768]{0:T(1024)} %param.27) | copy-start | bytes 9220
  144.4 137.4 %copy-start.62 = (f32[768]{0:T(1024)S(1)}, f32[768]{0:T(1024)}, u32[]{:S(2)}) copy-start(f32[768]{0:T(1024)} %param.28) | copy-start | bytes 9220
  144.4 215.9 %all-gather.9.cloned.1.call-start = ((), (), s32[]{:S(2)}) async-start(), calls=%async_computation.9 | async-start | bytes 4915200 | tf_op jit(solution)/shard_map/all_gather | solution.py:90
  281.4 255.8 %copy-start.5 = (f32[16,40,768]{2,1,0:T(8,128)}, f32[16,40,768]{2,1,0:T(8,128)S(1)}, u32[]{:S(2)}) copy-start(f32[16,40,768]{2,1,0:T(8,128)S(1)} %get-tuple-element.102) | copy-start | bytes 5898244
  281.4 255.8 %copy-start.45 = (f32[16,40]{1,0:T(8,128)}, f32[16,40]{1,0:T(8,128)S(1)}, u32[]{:S(2)}) copy-start(f32[16,40]{1,0:T(8,128)S(1)} %broadcast_multiply_fusion.9) | copy-start | bytes 7684
  281.8 255.4 %copy-start.51 = (f32[16,40]{1,0:T(8,128)}, f32[16,40]{1,0:T(8,128)S(1)}, u32[]{:S(2)}) copy-start(f32[16,40]{1,0:T(8,128)S(1)} %add_rsqrt_fusion.2) | copy-start | bytes 7684
  283.2 254.0 %reduce-scatter.10.cloned.1.call-start = ((), (), s32[]{:S(2)}) async-start(), calls=%async_computation.10 | async-start | bytes 9830400 | tf_op jit(solution)/shard_map/reduce_scatter | solution.py:98
  283.5 18.0 %copy-start.64 = (s32[16]{0:T(128)}, s32[16]{0:T(128)S(1)}, u32[]{:S(2)}) copy-start(s32[16]{0:T(128)S(1)} %reduce) | copy-start | bytes 196
  283.5 36.0 %copy-start.66 = (s32[16]{0:T(128)}, s32[16]{0:T(128)S(1)}, u32[]{:S(2)}) copy-start(s32[16]{0:T(128)S(1)} %fusion.111) | copy-start | bytes 196
  310.6 8.9 copy-start.56
  378.3 3.2 copy-start.2
  402.2 138.4 %copy-start.53 = (f32[768]{0:T(1024)S(1)}, f32[768]{0:T(1024)}, u32[]{:S(2)}) copy-start(f32[768]{0:T(1024)} %param.32) | copy-start | bytes 9220
  402.2 138.4 %copy-start.63 = (f32[768]{0:T(1024)S(1)}, f32[768]{0:T(1024)}, u32[]{:S(2)}) copy-start(f32[768]{0:T(1024)} %param.33) | copy-start | bytes 9220
  402.2 216.8 %all-gather.11.cloned.1.call-start = ((), (), s32[]{:S(2)}) async-start(), calls=%async_computation.11 | async-start | bytes 4915200 | tf_op jit(solution)/shard_map/all_gather | solution.py:188
  539.3 79.7 %copy-start.76 = (f32[768]{0:T(1024)S(1)}, f32[768]{0:T(1024)}, u32[]{:S(2)}) copy-start(f32[768]{0:T(1024)} %param.35) | copy-start | bytes 9220
  542.0 101.8 %copy-start.75 = (bf16[768,768]{1,0:T(8,128)(2,1)S(1)}, bf16[768,768]{1,0:T(8,128)(2,1)}, u32[]{:S(2)}) copy-start(bf16[768,768]{1,0:T(8,128)(2,1)} %param.36) | copy-start | bytes 3538948
  542.0 242.2 %reduce-scatter.12.cloned.1.call-start = ((), (), s32[]{:S(2)}) async-start(), calls=%async_computation.12 | async-start | bytes 9830400 | tf_op jit(solution)/shard_map/reduce_scatter | solution.py:191
  649.2 135.0 %copy-start.8 = (f32[16,40,768]{2,1,0:T(8,128)S(1)}, f32[16,40,768]{2,1,0:T(8,128)}, u32[]{:S(2)}) copy-start(f32[16,40,768]{2,1,0:T(8,128)} %copy-done.7) | copy-start | bytes 5898244
  649.2 137.6 %copy-start.57 = (f32[768]{0:T(1024)S(1)}, f32[768]{0:T(1024)}, u32[]{:S(2)}) copy-start(f32[768]{0:T(1024)} %param.37) | copy-start | bytes 9220
  649.2 217.8 %all-gather.13.cloned.1.call-start = ((), (), s32[]{:S(2)}) async-start(), calls=%async_computation.13 | async-start | bytes 4915200 | tf_op jit(solution)/shard_map/all_gather | solution.py:205
  789.9 231.4 %reduce-scatter.14.cloned.1.call-start = ((), (), s32[]{:S(2)}) async-start(), calls=%async_computation.14 | async-start | bytes 9830400 | tf_op jit(solution)/shard_map/reduce_scatter | solution.py:215
  886.4 135.0 %copy-start.18 = (bf16[16,40,768]{2,1,0:T(8,128)(2,1)S(1)}, bf16[16,40,768]{2,1,0:T(8,128)(2,1)}, u32[]{:S(2)}) copy-start(bf16[16,40,768]{2,1,0:T(8,128)(2,1)} %param.39) | copy-start | bytes 2949124
  886.4 135.0 %copy-start.68 = (f32[768]{0:T(1024)S(1)}, f32[768]{0:T(1024)}, u32[]{:S(2)}) copy-start(f32[768]{0:T(1024)} %param.38) | copy-start | bytes 9220
  886.4 219.6 %all-gather.15.cloned.1.call-start = ((), (), s32[]{:S(2)}) async-start(), calls=%async_computation.15 | async-start | bytes 4915200 | tf_op jit(solution)/shard_map/all_gather | solution.py:94
  1027.3 78.7 %copy-start.47 = (bf16[192,768]{1,0:T(8,128)(2,1)S(1)}, bf16[192,768]{1,0:T(8,128)(2,1)}, u32[]{:S(2)}) copy-start(bf16[192,768]{1,0:T(8,128)(2,1)} %param.31) | copy-start | bytes 884740
  1028.9 189.2 %reduce-scatter.16.cloned.1.call-start = ((), (), s32[]{:S(2)}) async-start(), calls=%async_computation.16 | async-start | bytes 4915200 | tf_op jit(solution)/shard_map/reduce_scatter | solution.py:117
  1112.6 20.0 %slice-start = ((s8[6291456]{0:T(1024)(128)(4,1)}), s8[2097152]{0:T(1024)(128)(4,1)S(1)}, s32[]{:S(2)}) async-start(s8[6291456]{0:T(1024)(128)(4,1)} %bitcast.202), calls=%async_computation.21 | async-start | bytes 4194304
  1117.0 15.6 slice-start.1
  1138.8 3.3 copy-start.50
  1146.6 71.5 %copy-start.6 = (f32[16,40,768]{2,1,0:T(8,128)S(1)}, f32[16,40,768]{2,1,0:T(8,128)}, u32[]{:S(2)}) copy-start(f32[16,40,768]{2,1,0:T(8,128)} %copy-done.5) | copy-start | bytes 5898244
  1146.6 71.5 %copy-start.46 = (f32[16,40]{1,0:T(8,128)S(1)}, f32[16,40]{1,0:T(8,128)}, u32[]{:S(2)}) copy-start(f32[16,40]{1,0:T(8,128)} %copy-done.45) | copy-start | bytes 7684
  1146.6 71.5 %copy-start.52 = (f32[16,40]{1,0:T(8,128)S(1)}, f32[16,40]{1,0:T(8,128)}, u32[]{:S(2)}) copy-start(f32[16,40]{1,0:T(8,128)} %copy-done.51) | copy-start | bytes 7684
  1146.6 71.5 %copy-start.55 = (f32[768]{0:T(1024)S(1)}, f32[768]{0:T(1024)}, u32[]{:S(2)}) copy-start(f32[768]{0:T(1024)} %param.27) | copy-start | bytes 9220
  1146.6 154.6 %all-gather.17.cloned.1.call-start = ((), (), s32[]{:S(2)}) async-start(), calls=%async_computation.17 | async-start | bytes 4915200 | tf_op jit(solution)/shard_map/all_gather | solution.py:94
  1224.3 231.7 %reduce-scatter.20.cloned.1.call-start = ((), (), s32[]{:S(2)}) async-start(), calls=%async_computation.19 | async-start | bytes 6225920 | tf_op jit(solution)/shard_map/reduce_scatter | solution.py:252
  1257.9 12.8 copy-start.65
  1257.9 12.8 copy-start.67
  1270.7 7.1 copy-start.10
  1277.7 5.0 copy-start.29
  1277.8 3.3 copy-start.33
  1286.8 181.2 %reduce-scatter.18.cloned.1.call-start = ((), (), s32[]{:S(2)}) async-start(), calls=%async_computation.18 | async-start | bytes 4915200 | tf_op jit(solution)/shard_map/reduce_scatter | solution.py:117
  1287.8 13.4 copy-start.49
  1323.7 5.1 copy-start.4
  1351.1 9.0 copy-start.39
  1367.3 251.5 %all-reduce.4.cloned.1.call-start = ((), (), s32[]{:S(2)}) async-start(), calls=%async_computation.20 | async-start | bytes 19660800 | tf_op jit(solution)/shard_map/psum | solution.py:291
  1367.5 8.1 copy-start.30
  1367.5 11.8 slice-start.2
  1375.7 3.7 slice-start.3
  1375.7 4.1 copy-start.32
  1383.1 3.0 copy-start.73
  1398.1 15.0 copy-start.58
  1398.2 15.0 copy-start.59
  1398.2 15.0 copy-start.60
  1398.2 15.0 copy-start.61
  1618.9 3.8 copy-start.41
  1618.9 4.6 copy-start.36
  1625.4 3.9 copy-start.1
  (33 other events, 63.3 us)
Sparse Core Ops, SparseCore 0:
  9.6 79.1 all-gather.6
  144.5 134.8 reduce-scatter.7
  283.3 76.9 all-gather.8
  402.3 134.8 reduce-scatter.9
  542.1 76.9 all-gather.10
  649.3 134.7 reduce-scatter.11
  790.1 76.9 all-gather.12
  886.5 134.8 reduce-scatter.13
  1029.0 76.9 all-gather.14
  1146.7 71.2 reduce-scatter.15
  1224.4 76.7 all-gather.16
  1303.4 88.0 reduce-scatter.19
  1393.8 74.1 reduce-scatter.17
  1473.9 144.8 all-reduce.3
where the time goes:
time: 1650 us; the launch traced here: 1640 us
  waiting for transfers between devices  1120 us (68%)
  matrix products  225 us (14%)
  local copies, waits for them, and re-layouts  170 us (10%)
  blocking collectives  57.1 us (3%)
  other arithmetic  43.3 us (3%)
    reduce_scatter x2, waiting for transfers between devices, scatter_out(): lax.psum_scatter(jnp.dot(inputs_all, weight, preferred_element_type=jnp.f...  269 us
    psum x1, waiting for transfers between devices, per_device(): lax.psum((self_project_grad, self_output_grad, cross_query_grad, cross_ke...  147 us
    reduce_scatter x1, waiting for transfers between devices, per_device(): lax.psum_scatter(back_term([(expand_low, expand_weight)]), 'mp', scatter_...  135 us
    reduce_scatter x1, waiting for transfers between devices, per_device(): lax.psum_scatter(jnp.dot(activated, shrink_weight, preferred_element_type...  135 us
    all_gather x2, waiting for transfers between devices, gather_rows(): return lax.all_gather(local_rows, 'mp', axis=0, tiled=True)  121 us
    all_gather x2, waiting for transfers between devices, gather_grads(): return lax.all_gather(local_grads, 'mp', axis=0, tiled=True)  82.3 us
    reduce_scatter x2, waiting for transfers between devices, scatter_back(): lax.psum_scatter(back_term(pairs).astype(jnp.bfloat16), 'mp', scatter_dim...  80.4 us
    all_gather x1, waiting for transfers between devices, per_device(): feed_all = lax.all_gather(feed_low, 'mp', axis=0, tiled=True)  77 us
  transfers between devices with their start and end apart: 14, of which 13 were waited for; matrix products, arithmetic and copies ran while one was open for 13% of the time, Pallas kernels for 0%

commit v1 on v0

v1 whole, which is shorter than its diff:
```python
import functools

import jax
import jax.numpy as jnp
from jax import lax
from jax.experimental import pallas as pl
from jax.experimental.pallas import tpu as pltpu
from jax.sharding import PartitionSpec as P

HEAD_DIM = 64
ROWS_MAX = 7
MESH = pl.DeviceIdType.MESH


def place():
    index = lax.axis_index("dp")
    plane = lax.axis_index("mp")
    y, x, c = index // 4, (index // 2) % 2, index % 2
    return index, plane, y, x, c


def partners(index, plane):
    core = (index + 1 - 2 * (index % 2), plane)
    across = (index + 2 - 4 * ((index // 2) % 2), plane)
    along = (index + 4 - 8 * (index // 4), plane)
    planes = [(index, lax.rem(plane + step, 4)) for step in (1, 2, 3)]
    return core, across, along, planes


def greet(peers):
    barrier = pltpu.get_barrier_semaphore()
    for peer in peers:
        pl.semaphore_signal(barrier, inc=1, device_id=peer, device_id_type=MESH)
    pl.semaphore_wait(barrier, len(peers))


def gather_kernel(chunks, count, *refs):
    shards, outs, wholes = refs[:count], refs[count : 2 * count], refs[2 * count : 3 * count]
    final_sem, local_sem, plane_send, plane_recv, near_send, near_recv, far_send, far_recv, core_send, core_recv = refs[3 * count :]
    index, plane, y, x, c = place()
    core, across, along, planes = partners(index, plane)
    greet([core, across, along] + planes)
    others = [lax.rem(plane + step, 4) for step in (1, 2, 3)]
    total = len(chunks)

    def send(source, target, sends, recvs, peer):
        copy = pltpu.make_async_remote_copy(
            src_ref=source, dst_ref=target, send_sem=sends, recv_sem=recvs, device_id=peer, device_id_type=MESH
        )
        copy.start()
        return copy

    copies = {}
    sent = []

    def keep(name, k, items):
        copies[name, k] = items
        sent.extend(items)

    def arrived(name, k):
        for copy in copies[name, k]:
            copy.wait_recv()

    def sizes(k):
        which, base, rows = chunks[k]
        return which, base, rows // 8, shards[which].shape[1] // 2

    def level(k):
        which, base, r, w = sizes(k)
        items = []
        for h, first in enumerate((x * 2 + y, y * 2 + x)):
            row = pl.multiple_of(base + (c * 4 + first) * r, 16)
            here = (pl.ds(row, r), pl.ds(h * w, w))
            for j, peer in enumerate(planes):
                items.append(
                    send(
                        shards[which].at[here],
                        wholes[which].at[(plane,) + here],
                        plane_send.at[k, h, j],
                        plane_recv.at[k, h, j],
                        peer,
                    )
                )
        keep("plane", k, items)

    def near(k):
        which, base, r, w = sizes(k)
        arrived("plane", k)
        if k + window < total:
            level(k + window)
        items = []
        for h, first in enumerate((x * 2 + y, y * 2 + x)):
            row = pl.multiple_of(base + (c * 4 + first) * r, 16)
            for j, other in enumerate(others):
                piece = wholes[which].at[other, pl.ds(row, r), pl.ds(h * w, w)]
                items.append(send(piece, piece, near_send.at[k, h, j], near_recv.at[k, h, j], (along, across)[h]))
        keep("near", k, items)

    def far(k):
        which, base, r, w = sizes(k)
        arrived("near", k)
        items = []
        for h, first in enumerate((x, y)):
            row = pl.multiple_of(base + (c * 4 + first * 2) * r, 16)
            for j, other in enumerate(others):
                piece = wholes[which].at[other, pl.ds(row, 2 * r), pl.ds(h * w, w)]
                items.append(send(piece, piece, far_send.at[k, h, j], far_recv.at[k, h, j], (across, along)[h]))
        keep("far", k, items)

    def cross(k):
        which, base, r, w = sizes(k)
        arrived("far", k)
        row = pl.multiple_of(base + c * 4 * r, 16)
        items = []
        for j, other in enumerate(others):
            piece = wholes[which].at[other, pl.ds(row, 4 * r), :]
            items.append(send(piece, piece, core_send.at[k, j], core_recv.at[k, j], core))
        keep("core", k, items)

    final = []

    def end(k):
        which, base, r, w = sizes(k)
        arrived("core", k)
        if k + 1 == total or chunks[k + 1][0] != which:
            local[which].wait()
            copy = pltpu.make_async_copy(wholes[which], outs[which], final_sem.at[which])
            copy.start()
            final.append(copy)

    window, gap = 3, 2
    for k in range(window):
        level(k)
    local = []
    for which in range(count):
        copy = pltpu.make_async_copy(shards[which], wholes[which].at[plane], local_sem.at[which])
        copy.start()
        local.append(copy)
    stages = [near, far, cross, end]
    for t in range(total + gap * (len(stages) - 1)):
        for s in reversed(range(len(stages))):
            if 0 <= t - gap * s < total:
                stages[s](t - gap * s)
    for copy in sent:
        copy.wait_send()
    for copy in final:
        copy.wait()


def gather_weights(shards, chunks, collective_id=0):
    count = len(shards)
    total = len(chunks)
    dma = pltpu.SemaphoreType.DMA
    return pl.pallas_call(
        functools.partial(gather_kernel, chunks, count),
        out_shape=[jax.ShapeDtypeStruct((4,) + s.shape, s.dtype) for s in shards],
        in_specs=[pl.BlockSpec(memory_space=pl.ANY)] * count,
        out_specs=[pl.BlockSpec(memory_space=pl.ANY)] * count,
        scratch_shapes=[pltpu.VMEM((4,) + s.shape, s.dtype) for s in shards]
        + [dma((count,))] * 2 + [dma((total, 2, 3))] * 6 + [dma((total, 3))] * 2,
        compiler_params=pltpu.CompilerParams(
            collective_id=collective_id, has_side_effects=True, vmem_limit_bytes=60 << 20
        ),
        name="gather_weights",
    )(*shards)


def reduce_kernel(count, *refs):
    grads, sums = refs[:count], refs[count : 2 * count]
    rest = refs[2 * count :]
    bufs = [rest[i * count : (i + 1) * count] for i in range(6)]
    mine, core_in, near_in, far_in, plane_in, done = bufs
    (local_sem, core_send, core_recv, near_send, near_recv, far_send, far_recv, plane_send, plane_recv,
     out_near_send, out_near_recv, out_far_send, out_far_recv, out_core_send, out_core_recv, final_sem) = rest[6 * count :]
    index, plane, y, x, c = place()
    core, across, along, planes = partners(index, plane)
    greet([core, across, along] + planes)
    others = [lax.rem(plane + step, 4) for step in (1, 2, 3)]

    def send(source, target, sends, recvs, peer):
        copy = pltpu.make_async_remote_copy(
            src_ref=source, dst_ref=target, send_sem=sends, recv_sem=recvs, device_id=peer, device_id_type=MESH
        )
        copy.start()
        return copy

    def blocks(k):
        _, rows, width = grads[k].shape
        return rows // 8, width // 2

    def add(total, total_row, total_col, part, part_col, rows, cols):
        step = 16
        @pl.loop(0, rows // step)
        def _(i):
            for shard in range(4):
                here = (shard, pl.ds(pl.multiple_of(total_row + i * step, 16), step), pl.ds(total_col, cols))
                there = (shard, pl.ds(pl.multiple_of(i * step, 16), step), pl.ds(part_col, cols))
                total[here] = (total[here].astype(jnp.float32) + part[there].astype(jnp.float32)).astype(jnp.bfloat16)

    copies = {}
    sends = []

    def keep(name, k, items):
        copies[name, k] = items
        sends.extend(items)

    def arrived(name, k):
        for copy in copies[name, k]:
            copy.wait_recv()

    local = {}

    def begin(k):
        r, w = blocks(k)
        theirs = pl.multiple_of((1 - c) * 4 * r, 16)
        ours = pl.multiple_of(c * 4 * r, 16)
        keep("core", k, [send(grads[k].at[:, pl.ds(theirs, 4 * r), :], core_in[k], core_send.at[k], core_recv.at[k], core)])
        local[k] = pltpu.make_async_copy(grads[k].at[:, pl.ds(ours, 4 * r), :], mine[k], local_sem.at[k])
        local[k].start()

    def near(k):
        r, w = blocks(k)
        local[k].wait()
        arrived("core", k)
        add(mine[k], 0, 0, core_in[k], 0, 4 * r, 2 * w)
        items = []
        for h, (bit, peer) in enumerate([(x, across), (y, along)]):
            row = pl.multiple_of((1 - bit) * 2 * r, 16)
            items.append(send(mine[k].at[:, pl.ds(row, 2 * r), pl.ds(h * w, w)], near_in[k].at[h], near_send.at[k, h], near_recv.at[k, h], peer))
        keep("near", k, items)

    def far(k):
        r, w = blocks(k)
        arrived("near", k)
        items = []
        for h, (bit, second, peer) in enumerate([(x, y, along), (y, x, across)]):
            row = bit * 2 * r
            add(mine[k], row, h * w, near_in[k].at[h], 0, 2 * r, w)
            row = pl.multiple_of(row + (1 - second) * r, 16)
            items.append(send(mine[k].at[:, pl.ds(row, r), pl.ds(h * w, w)], far_in[k].at[h], far_send.at[k, h], far_recv.at[k, h], peer))
        keep("far", k, items)

    def places(k):
        r, w = blocks(k)
        return [((x * 2 + y) * r, 0), ((y * 2 + x) * r, w)]

    def level(k):
        r, w = blocks(k)
        arrived("far", k)
        items = []
        for h, (row, col) in enumerate(places(k)):
            add(mine[k], row, col, far_in[k].at[h], 0, r, w)
            row = pl.multiple_of(row, 16)
            for j in range(3):
                items.append(send(mine[k].at[others[j], pl.ds(row, r), pl.ds(col, w)], plane_in[k].at[h, j], plane_send.at[k, h, j], plane_recv.at[k, h, j], planes[j]))
        keep("plane", k, items)

    def out_near(k):
        r, w = blocks(k)
        arrived("plane", k)
        items = []
        for h, (row, col) in enumerate(places(k)):
            @pl.loop(0, r // 16)
            def _(i):
                step = pl.multiple_of(i * 16, 16)
                total = mine[k][plane, pl.ds(pl.multiple_of(row + i * 16, 16), 16), pl.ds(col, w)].astype(jnp.float32)
                for j in range(3):
                    total = total + plane_in[k][h, j, pl.ds(step, 16), :].astype(jnp.float32)
                done[k][pl.ds(pl.multiple_of(c * 4 * r + row + i * 16, 16), 16), pl.ds(col, w)] = total.astype(jnp.bfloat16)
            piece = done[k].at[pl.ds(pl.multiple_of(c * 4 * r + row, 16), r), pl.ds(col, w)]
            items.append(send(piece, piece, out_near_send.at[k, h], out_near_recv.at[k, h], (along, across)[h]))
        keep("out_near", k, items)

    def out_far(k):
        r, w = blocks(k)
        arrived("out_near", k)
        items = []
        for h, (bit, peer) in enumerate([(x, across), (y, along)]):
            piece = done[k].at[pl.ds(pl.multiple_of((c * 4 + bit * 2) * r, 16), 2 * r), pl.ds(h * w, w)]
            items.append(send(piece, piece, out_far_send.at[k, h], out_far_recv.at[k, h], peer))
        keep("out_far", k, items)

    def out_core(k):
        r, w = blocks(k)
        arrived("out_far", k)
        piece = done[k].at[pl.ds(pl.multiple_of(c * 4 * r, 16), 4 * r), :]
        keep("out_core", k, [send(piece, piece, out_core_send.at[k], out_core_recv.at[k], core)])

    final = []

    def end(k):
        arrived("out_core", k)
        copy = pltpu.make_async_copy(done[k], sums[k], final_sem.at[k])
        copy.start()
        final.append(copy)

    stages = [begin, near, far, level, out_near, out_far, out_core, end]
    for t in range(count + len(stages) - 1):
        for s in reversed(range(len(stages))):
            if 0 <= t - s < count:
                stages[s](t - s)
    for copy in sends:
        copy.wait_send()
    for copy in final:
        copy.wait()


def reduce_grads(grads, collective_id=1):
    count = len(grads)
    bf = jnp.bfloat16
    shapes = [g.shape for g in grads]
    scratch = []
    scratch += [pltpu.VMEM((4, R // 2, W), bf) for _, R, W in shapes]
    scratch += [pltpu.VMEM((4, R // 2, W), bf) for _, R, W in shapes]
    scratch += [pltpu.VMEM((2, 4, R // 4, W // 2), bf) for _, R, W in shapes]
    scratch += [pltpu.VMEM((2, 4, R // 8, W // 2), bf) for _, R, W in shapes]
    scratch += [pltpu.VMEM((2, 3, R // 8, W // 2), bf) for _, R, W in shapes]
    scratch += [pltpu.VMEM((R, W), bf) for _, R, W in shapes]
    D = pltpu.SemaphoreType.DMA
    scratch += [D((count,))] * 3 + [D((count, 2))] * 4 + [D((count, 2, 3))] * 2 + [D((count, 2))] * 4 + [D((count,))] * 3
    return pl.pallas_call(
        functools.partial(reduce_kernel, count),
        out_shape=[jax.ShapeDtypeStruct(s[1:], bf) for s in shapes],
        in_specs=[pl.BlockSpec(memory_space=pl.ANY)] * count,
        out_specs=[pl.BlockSpec(memory_space=pl.ANY)] * count,
        scratch_shapes=scratch,
        compiler_params=pltpu.CompilerParams(collective_id=collective_id, has_side_effects=True, vmem_limit_bytes=60 << 20),
        name="reduce_grads",
    )(*grads)


highest = lax.Precision.HIGHEST


def rows_structure(counts, group_rows):
    row_ends = jnp.cumsum(counts)
    starts = row_ends - counts
    row_index = jnp.arange(group_rows, dtype=jnp.int32)[:, None]
    member = (row_index >= starts[None, :]) & (row_index < row_ends[None, :])
    caption = jnp.any(row_index == starts[None, :], axis=1)
    return (member, caption)


def normalize(hidden):
    center = hidden - jnp.mean(hidden, axis=-1, keepdims=True)
    inverse = lax.rsqrt(jnp.mean(center * center, axis=-1, keepdims=True) + 1e-06)
    return (center * inverse, inverse)


def norm_back(upstream, scaled, inverse, norm_gain):
    scaled_grad = upstream * norm_gain
    return inverse * (
        scaled_grad
        - jnp.mean(scaled_grad, axis=-1, keepdims=True)
        - scaled * jnp.mean(scaled_grad * scaled, axis=-1, keepdims=True)
    )


def split_heads(values):
    return values.reshape(values.shape[0], values.shape[1], values.shape[2] // HEAD_DIM, HEAD_DIM)


def masked_scores(queries, key_rows, allowed):
    scores = jnp.einsum(
        "gqhe,gkhe->ghqk",
        split_heads(queries),
        split_heads(key_rows),
        preferred_element_type=jnp.float32,
    ) * HEAD_DIM ** (-0.5)
    return jnp.where(allowed[:, None, None, :], scores, -1000000000.0)


def attend(queries, key_rows, value_rows, allowed):
    scores = masked_scores(queries, key_rows, allowed)
    row_peak = jnp.max(scores, axis=-1, keepdims=True)
    raised = jnp.exp(scores - row_peak)
    row_total = jnp.sum(raised, axis=-1, keepdims=True)
    weights = (raised / row_total).astype(jnp.bfloat16)
    context = jnp.einsum(
        "ghqk,gkhe->gqhe", weights, split_heads(value_rows), preferred_element_type=jnp.float32
    )
    return (context.reshape(queries.shape), row_peak + jnp.log(row_total))


def attend_back(queries, key_rows, value_rows, allowed, row_lse, context_grad):
    scores = masked_scores(queries, key_rows, allowed)
    probs = jnp.exp(scores - row_lse)
    weights = probs.astype(jnp.bfloat16)
    grad_heads = split_heads(context_grad)
    prob_grad = jnp.einsum(
        "gqhe,gkhe->ghqk", grad_heads, split_heads(value_rows), preferred_element_type=jnp.float32
    )
    score_low = (probs * (prob_grad - jnp.sum(probs * prob_grad, axis=-1, keepdims=True))).astype(
        jnp.bfloat16
    )
    query_grad = jnp.einsum(
        "ghqk,gkhe->gqhe", score_low, split_heads(key_rows), preferred_element_type=jnp.float32
    ) * HEAD_DIM ** (-0.5)
    key_grad = jnp.einsum(
        "ghqk,gqhe->gkhe", score_low, split_heads(queries), preferred_element_type=jnp.float32
    ) * HEAD_DIM ** (-0.5)
    value_grad = jnp.einsum(
        "ghqk,gqhe->gkhe", weights, grad_heads, preferred_element_type=jnp.float32
    )
    return (
        query_grad.reshape(queries.shape),
        key_grad.reshape(key_rows.shape),
        value_grad.reshape(value_rows.shape),
    )

def most_images(rows, group_rows, group_images):
    best = 1
    for touched in range(2, min(rows, group_images) + 1):
        inner, outer = touched - 2, group_images - touched + 2
        if inner + 2 <= rows and group_rows - (rows - 2) <= ROWS_MAX * outer:
            best = touched
    return best


def gather_shards(shards, chunks, own):
    if own:
        return gather_weights(shards, chunks)
    return [lax.all_gather(shard, "mp", axis=0) for shard in shards]


def reduce_shards(grads, own):
    if own:
        return [total.astype(jnp.float32) for total in reduce_grads(grads)]
    return [
        lax.psum(lax.psum_scatter(grad.astype(jnp.float32), "mp", scatter_dimension=0, tiled=True)[0], "dp")
        for grad in grads
    ]


def spread(inputs, blocks):
    result = lax.dot_general(inputs, blocks, (((1,), (2,)), ((), ())), preferred_element_type=jnp.float32)
    return result.reshape(inputs.shape[0], -1)


def join(inputs, blocks):
    split = inputs.reshape(inputs.shape[0], blocks.shape[0], blocks.shape[1])
    return lax.dot_general(split, blocks, (((1, 2), (0, 1)), ((), ())), preferred_element_type=jnp.float32)


def outer(left, right, parts):
    result = lax.dot_general(left, right, (((0,), (0,)), ((), ())), preferred_element_type=jnp.float32)
    return result.astype(jnp.bfloat16).reshape(parts, left.shape[1] // parts, right.shape[1])


def per_device(
    tokens, patches, image_rows, row_lengths, box_mask, self_project, self_output, first_gain, first_shift, cross_query,
    cross_keyval, cross_output, second_gain, second_shift, expand_weight, expand_bias, shrink_weight, third_gain,
    third_shift, cotangent, *, parts, own,
):
    bf16 = jnp.bfloat16
    rows, slots, width = tokens.shape
    group_rows = row_lengths.shape[0]
    group_images, cells = patches.shape[0], patches.shape[1]
    window = most_images(rows, group_rows, group_images)
    plane = lax.axis_index("mp")

    inner = self_output.shape[0]
    small = jnp.concatenate(
        [self_project[c].T for c in range(3)] + [self_output, cross_query.T, cross_output], axis=0
    )
    keyval = jnp.concatenate([cross_keyval[0].T, cross_keyval[1].T], axis=0)
    chunks = [(0, i * 384, 384) for i in range(3)] + [(1, 0, 384)]
    chunks += [(2, i * 384, 384) for i in range(2)] + [(3, i * 384, 384) for i in range(2)]
    small, keyval, expand, shrink = gather_shards([small, keyval, expand_weight.T, shrink_weight], chunks, own)
    project = [small[:, c * inner : (c + 1) * inner] for c in range(3)]
    self_out, query_weight, cross_out = (small[:, c * inner : (c + 1) * inner] for c in range(3, 6))
    key_weight, value_weight = keyval[:, :inner], keyval[:, inner:]
    bias = lax.all_gather(expand_bias, "mp", axis=0, tiled=True)

    member, caption = rows_structure(image_rows[0], group_rows)
    member = lax.dynamic_slice_in_dim(member, plane * rows, rows, 0)
    caption = lax.dynamic_slice_in_dim(caption, plane * rows, rows, 0)
    lengths = lax.dynamic_slice_in_dim(row_lengths, plane * rows, rows, 0)
    boxes = lax.dynamic_slice_in_dim(box_mask, plane * rows, rows, 0)
    start = jnp.minimum(jnp.argmax(member[0]).astype(jnp.int32), group_images - window)
    member = lax.dynamic_slice_in_dim(member, start, window, 1)
    member_low, member_full = member.astype(bf16), member.astype(jnp.float32)
    near = lax.dynamic_slice_in_dim(patches, start, window, 0).reshape(window * cells, -1)
    key_ok = jnp.arange(slots, dtype=jnp.int32)[None, :] < lengths[:, None]
    cross_ok = caption[:, None] | (boxes > 0)

    text = tokens.reshape(rows * slots, width)
    shape = (rows, slots, width)
    queries, key_rows, value_rows = (spread(text, weight).astype(bf16).reshape(shape) for weight in project)
    self_context, self_lse = attend(queries, key_rows, value_rows, key_ok)
    self_low = self_context.astype(bf16).reshape(text.shape)
    after_self = text.astype(jnp.float32) + join(self_low, self_out)
    first_scaled, first_inverse = normalize(after_self)
    first_value = first_scaled * first_gain + first_shift
    first_low = first_value.astype(bf16)
    cross_queries = spread(first_low, query_weight).astype(bf16).reshape(shape)
    image_keys = spread(near, key_weight).astype(bf16).reshape(window, cells, width)
    image_values = spread(near, value_weight).astype(bf16).reshape(window, cells, width)
    row_keys, row_values = (
        jnp.einsum("gi,ipe->gpe", member_low, part, preferred_element_type=jnp.float32).astype(bf16)
        for part in (image_keys, image_values)
    )
    cross_context, cross_lse = attend(cross_queries, row_keys, row_values, cross_ok)
    cross_low = cross_context.astype(bf16).reshape(text.shape)
    after_cross = first_value + join(cross_low, cross_out)
    second_scaled, second_inverse = normalize(after_cross)
    second_value = second_scaled * second_gain + second_shift
    second_low = second_value.astype(bf16)
    expanded = spread(second_low, expand) + bias
    activated = jax.nn.gelu(expanded, approximate=False).astype(bf16)
    after_feed = second_value + join(activated, shrink)
    third_scaled, third_inverse = normalize(after_feed)
    joined = (third_scaled * third_gain + third_shift).astype(bf16)

    upstream = cotangent.reshape(text.shape).astype(jnp.float32)
    third_gain_grad = jnp.sum(upstream * third_scaled, axis=0)
    third_shift_grad = jnp.sum(upstream, axis=0)
    feed_grad = norm_back(upstream, third_scaled, third_inverse, third_gain)
    feed_low = feed_grad.astype(bf16)
    gelu_back = jax.vjp(lambda inner: jax.nn.gelu(inner, approximate=False), expanded)[1]
    shrink_grad = outer(activated, feed_low, parts)
    expand_low = gelu_back(spread(feed_low, shrink))[0].astype(bf16)
    expand_bias_grad = jnp.sum(expand_low.astype(jnp.float32), axis=0)
    expand_grad = outer(expand_low, second_low, parts)
    second_up = feed_grad + join(expand_low, expand)
    second_gain_grad = jnp.sum(second_up * second_scaled, axis=0)
    second_shift_grad = jnp.sum(second_up, axis=0)
    cross_grad = norm_back(second_up, second_scaled, second_inverse, second_gain)
    cross_grad_low = cross_grad.astype(bf16)
    cross_output_grad = outer(cross_low, cross_grad_low, parts)
    context_low = spread(cross_grad_low, cross_out).astype(bf16).reshape(shape)
    cross_qpart, cross_kpart, cross_vpart = attend_back(
        cross_queries, row_keys, row_values, cross_ok, cross_lse, context_low
    )
    cross_query_low = cross_qpart.astype(bf16).reshape(text.shape)
    key_low, value_low = (
        jnp.einsum("gi,gpe->ipe", member_full, part, precision=highest).astype(bf16).reshape(window * cells, width)
        for part in (cross_kpart, cross_vpart)
    )
    cross_query_grad = outer(cross_query_low, first_low, parts)
    key_weight_grad, value_weight_grad = outer(key_low, near, parts), outer(value_low, near, parts)
    patch_part = (join(key_low, key_weight) + join(value_low, value_weight)).astype(bf16)
    patch_part = patch_part.reshape(window, cells, -1)
    patch_whole = lax.dynamic_update_slice_in_dim(jnp.zeros(patches.shape, bf16), patch_part, start, 0)
    patch_grad = lax.psum_scatter(patch_whole, "mp", scatter_dimension=2, tiled=True).astype(jnp.float32)
    first_up = cross_grad + join(cross_query_low, query_weight)
    first_gain_grad = jnp.sum(first_up * first_scaled, axis=0)
    first_shift_grad = jnp.sum(first_up, axis=0)
    self_grad = norm_back(first_up, first_scaled, first_inverse, first_gain)
    self_grad_low = self_grad.astype(bf16)
    self_output_grad = outer(self_low, self_grad_low, parts)
    self_context_low = spread(self_grad_low, self_out).astype(bf16).reshape(shape)
    part_low = [
        part.astype(bf16).reshape(text.shape)
        for part in attend_back(queries, key_rows, value_rows, key_ok, self_lse, self_context_low)
    ]
    project_grads = [outer(part, text, parts) for part in part_low]
    text_grad = self_grad + sum(join(part, weight) for part, weight in zip(part_low, project))

    small_grad = jnp.concatenate(project_grads + [self_output_grad, cross_query_grad, cross_output_grad], axis=1)
    keyval_grad = jnp.concatenate([key_weight_grad, value_weight_grad], axis=1)
    small_sum, keyval_sum, expand_sum, shrink_sum = reduce_shards([small_grad, keyval_grad, expand_grad, shrink_grad], own)
    cuts = [small_sum[c * inner : (c + 1) * inner] for c in range(6)]
    vectors = lax.psum(
        jnp.concatenate(
            [
                expand_bias_grad, first_gain_grad, first_shift_grad, second_gain_grad, second_shift_grad,
                third_gain_grad, third_shift_grad,
            ]
        ),
        ("dp", "mp"),
    )
    hidden = expand_bias_grad.shape[0]
    bias_grad = lax.dynamic_slice_in_dim(vectors, plane * (hidden // parts), hidden // parts, 0)
    norms = [vectors[hidden + i * width : hidden + (i + 1) * width] for i in range(6)]
    return (
        joined.reshape(shape),
        text_grad.reshape(shape),
        patch_grad,
        jnp.stack([cut.T for cut in cuts[:3]]),
        cuts[3],
        norms[0],
        norms[1],
        cuts[4].T,
        jnp.stack([keyval_sum[:inner].T, keyval_sum[inner:].T]),
        cuts[5],
        norms[2],
        norms[3],
        expand_sum.T,
        bias_grad,
        shrink_sum,
        norms[4],
        norms[5],
    )


def solution(mesh):
    parts = mesh.shape["mp"]
    own = mesh.shape["dp"] == 8 and parts == 4
    return jax.shard_map(
        functools.partial(per_device, parts=parts, own=own),
        mesh=mesh,
        in_specs=(
            P(("dp", "mp"), None, None),
            P("dp", None, None),
            P("dp", None),
            P("dp"),
            P("dp", None),
            P(None, None, "mp"),
            P("mp", None),
            P(),
            P(),
            P(None, "mp"),
            P(None, None, "mp"),
            P("mp", None),
            P(),
            P(),
            P(None, "mp"),
            P("mp"),
            P("mp", None),
            P(),
            P(),
            P(("dp", "mp"), None, None),
        ),
        out_specs=(
            P(("dp", "mp"), None, None),
            P(("dp", "mp"), None, None),
            P("dp", None, "mp"),
            P(None, None, "mp"),
            P("mp", None),
            P(),
            P(),
            P(None, "mp"),
            P(None, None, "mp"),
            P("mp", None),
            P(),
            P(),
            P(None, "mp"),
            P("mp"),
            P("mp", None),
            P(),
            P(),
        ),
        check_vma=False,
    )
```

time: 1650 us -> 920 us (0.56)
  waiting for transfers between devices: 1120 us -> 0.02 us
  Pallas kernels: 0 us -> 216 us
  local copies, waits for them, and re-layouts: 170 us -> 328 us
  other arithmetic: 43.3 us -> 80.6 us
    reduce_scatter x7 -> x1, waiting for transfers between devices: 620 us -> 0.01 us  [per_device(): lax.psum_scatter(patch_whole, 'mp', scatter_dimension=2, tiled=True)]
    all_gather x6 -> x0, waiting for transfers between devices: 357 us -> none  [the longest x2 121 us: gather_rows(): return lax.all_gather(local_rows, 'mp', axis=0, tiled=True)]
    pallas_call x0 -> x2, Pallas kernels: none -> 216 us  [the longest x1 127 us: reduce_grads(): pl.pallas_call(functools.partial(reduce_kernel, count), out_shape=[jax.Sh...]
    psum x1 -> x0, waiting for transfers between devices: 147 us -> none  [per_device(): lax.psum((self_project_grad, self_output_grad, cross_query_grad, cross_ke...]
    convert_element_type x20 -> x38, local copies, waits for them, and re-layouts: 88.1 us -> 168 us  [the longest x12 49.2 us: per_device(): part.astype(bf16).reshape(text.shape)]
    dynamic_update_slice x0 -> x1, local copies, waits for them, and re-layouts: none -> 43.2 us  [per_device(): lax.dynamic_update_slice_in_dim(jnp.zeros(patches.shape, bf16), patch_par...]
    convert_element_type x5 -> x6, other arithmetic: 7.28 us -> 34.6 us  [the longest x1 19 us: per_device(): activated = jax.nn.gelu(expanded, approximate=False).astype(bf16)]
    dot_general x0 -> x4, local copies, waits for them, and re-layouts: none -> 19.9 us  [the longest x2 18.5 us: spread(): lax.dot_general(inputs, blocks, (((1,), (2,)), ((), ())), preferred_eleme...]
  transfers between devices with their start and end apart: 14 -> 1, of which waited for: 13 -> 0; matrix products, arithmetic and copies ran while one was open for 13% -> 27% of each run, Pallas kernels for 0% -> 14%
where the time goes in v1:
time: 920 us; the launch traced here: 910 us
  local copies, waits for them, and re-layouts  328 us (36%)
  Pallas kernels  216 us (23%)
  matrix products  216 us (23%)
  other arithmetic  80.6 us (9%)
  blocking collectives  54 us (6%)
  between operations  16.2 us (2%)
    pallas_call x1, Pallas kernels, reduce_grads(): pl.pallas_call(functools.partial(reduce_kernel, count), out_shape=[jax.Sh...  127 us
    pallas_call x1, Pallas kernels, gather_weights(): pl.pallas_call(functools.partial(gather_kernel, chunks, count), out_shape...  88.7 us
    dot_general x10, matrix products, spread(): lax.dot_general(inputs, blocks, (((1,), (2,)), ((), ())), preferred_eleme...  50.3 us
    convert_element_type x12, local copies, waits for them, and re-layouts, per_device(): part.astype(bf16).reshape(text.shape)  49.2 us
    dot_general x10, matrix products, join(): lax.dot_general(split, blocks, (((1, 2), (0, 1)), ((), ())), preferred_el...  48.2 us
    dot_general x10, matrix products, outer(): lax.dot_general(left, right, (((0,), (0,)), ((), ())), preferred_element_...  43.6 us
    dynamic_update_slice x1, local copies, waits for them, and re-layouts, per_device(): lax.dynamic_update_slice_in_dim(jnp.zeros(patches.shape, bf16), patch_par...  43.2 us
    psum x1, blocking collectives, per_device(): lax.psum(jnp.concatenate([expand_bias_grad, first_gain_grad, first_shift_...  40.2 us
  transfers between devices with their start and end apart: 1, of which 0 were waited for; matrix products, arithmetic and copies ran while one was open for 27% of the time, Pallas kernels for 14%

profile of v1, /device:TPU:0, one launch (start us, length us, event | category | flops | bytes accessed | tf_op | source)
XLA Modules:
  0.0 910.4 jit_solution(853075130246438955)
XLA Ops:
  18.4 88.7 %gather_weights.1 = (bf16[4,1152,768]{2,1,0:T(8,128)(2,1)}, bf16[4,384,1024]{2,1,0:T(8,128)(2,1)}, bf16[4,768,768]{2,1,0:T(8,128)(2,1)}, bf16[4,768,768]{2,1,0:T(8,128)(2,1)}) custom-call(bf16[1152,768]{1,0:T(8,128)(2,1)} %copy-done.36, bf16[384,1024]{1,0:T(8,128)(2,1)} %pad_maximum_fusion.3.refs_1_, bf16[768,768]{1,0:T(8,128)(2,1)} %bitcast.323, ...), custom_call_target="tpu_custom_call" | custom-call | tf_op jit(solution)/shard_map/gather_weights/pallas_call | solution.py:154
  117.4 13.8 %all-gather = f32[4,1,768]{2,1,0:T(1,128)S(1)} all-gather(f32[1,1,768]{2,1,0:T(1,128)S(1)} %reshape.336), channel_id=1, replica_groups=mesh['dp'=8,'mp'=4] {'mp'}, dimensions={0}, use_global_device_ids=true | all-gather | bytes 15360 | tf_op jit(solution)/shard_map/all_gather | solution.py:473
  131.9 4.8 constant_dynamic-slice_fusion
  144.4 3.9 convolution_convert_fusion.3
  153.6 9.2 %copy.199 = bf16[16,145,768]{1,2,0:T(8,128)(2,1)} copy(bf16[16,145,768]{2,0,1:T(8,128)(2,1)} %fusion.40) | data formatting | bytes 7127040 | tf_op jit(solution)/shard_map/convert_element_type | solution.py:500
  162.8 5.8 reshape.369
  172.0 6.8 reshape.370
  178.8 3.8 copy.190
  182.6 5.5 reshape.371
  188.1 4.8 copy.191
  201.5 4.0 copy.247
  205.5 4.8 reshape.363
  218.2 5.8 reshape.372
  227.3 6.2 convolution_convert_fusion.2
  238.6 9.3 %copy.202 = bf16[16,145,768]{1,2,0:T(8,128)(2,1)} copy(bf16[16,145,768]{2,0,1:T(8,128)(2,1)} %fusion.43) | data formatting | bytes 7127040 | tf_op jit(solution)/shard_map/convert_element_type | solution.py:500
  248.7 5.4 fusion.35
  257.3 4.7 convert_bitcast_fusion.2
  262.0 4.0 copy.248
  266.0 4.4 reshape.364
  274.3 7.6 fusion.59
  281.9 17.3 %fusion = f32[640,4,768]{2,0,1:T(8,128)S(1)} fusion(f32[640,4,768]{2,0,1:T(8,128)S(1)} %get-tuple-element.152, f32[4,768]{1,0:T(4,128)S(1)} %bitcast.341, u8[640,768]{1,0:T(8,128)(4,1)S(1)} %get-tuple-element.104, u8[640,768]{1,0:T(8,128)(4,1)S(1)} %get-tuple-element.103), kind=kLoop, calls=%fused_computation.2 | loop fusion | flops 133693440 | bytes 16723968 | tf_op jit(solution)/shard_map/erfc | solution.py:510
  299.3 8.7 fusion.130
  312.6 13.9 %convert_reduce_fusion = (f32[4,768]{1,0:T(4,128)}, bf16[640,4,768]{2,0,1:T(8,128)(2,1)S(1)}, f32[640,4,768]{2,0,1:T(8,128)}) fusion(f32[640,4,768]{2,0,1:T(8,128)} %copy-done.25, f32[640,4,768]{2,0,1:T(8,128)} %copy-done.4, f32[4,768]{1,0:T(4,128)S(1)} %bitcast.343, bf16[4,768,768]{2,1,0:T(8,128)(2,1)} %get-tuple-element.30, ...), kind=kOutput, calls=%fused_computation.19 | convolution fusion | flops 3053810688 | bytes 34234368 | tf_op jit(solution)/shard_map/dot_general | solution.py:436
  326.6 4.2 multiply_reduce_fusion.2
  335.0 5.6 reshape.373
  344.4 7.5 multiply_reduce_fusion
  351.9 8.1 fusion.23
  359.9 6.0 multiply_convert_fusion.1
  365.9 6.3 broadcast_multiply_fusion
  372.3 11.6 %copy.225 = f32[16,145,768]{2,0,1:T(8,128)} copy(f32[16,145,768]{1,2,0:T(8,128)} %bitcast.316) | data formatting | bytes 14254080 | tf_op jit(solution)/shard_map/reshape | solution.py:407
  383.9 6.2 fusion.102
  390.8 4.4 reshape_reshape.4
  395.2 7.4 fusion.38
  402.6 11.6 %copy.230 = f32[16,145,768]{2,0,1:T(8,128)} copy(f32[16,145,768]{1,2,0:T(8,128)} %bitcast.315) | data formatting | bytes 14254080 | tf_op jit(solution)/shard_map/reshape | solution.py:408
  414.2 6.0 fusion.100
  421.0 4.3 reshape_reshape.5
  425.3 8.2 fusion.22
  436.3 4.0 copy.233
  443.1 43.2 %dynamic_update_slice.3 = bf16[16,145,1024]{2,0,1:T(8,128)(2,1)} dynamic-update-slice(bf16[16,145,1024]{2,0,1:T(8,128)(2,1)} %broadcast_in_dim.38, bf16[10,145,1024]{2,0,1:T(8,128)(2,1)} %copy.233, s32[]{:T(128)S(6)} %select_n.35, s32[]{:T(128)} %constant.48.clone.1, s32[]{:T(128)} %constant.48.clone.1) | dynamic-update-slice | bytes 5939204 | tf_op jit(solution)/shard_map/dynamic_update_slice | solution.py:544
  486.3 5.8 fusion.64
  495.8 4.8 reshape.365
  500.6 4.8 multiply_reduce_fusion.3
  509.7 5.6 reshape.374
  515.3 5.2 copy.211
  520.5 5.0 multiply_reduce_fusion.1
  534.5 5.1 copy.250
  543.3 5.0 copy.251
  551.9 5.0 copy.252
  556.9 3.8 copy.221
  570.7 3.9 bitcast_convert_fusion.1
  574.6 9.2 %copy.240 = f32[640,4,768]{0,2,1:T(8,128)} copy(f32[640,4,768]{2,0,1:T(8,128)} %copy-done.4) | data formatting | bytes 15728640 | tf_op jit(solution)/shard_map/dot_general | solution.py:436
  583.8 5.8 reshape.367
  589.6 4.4 reshape.366
  594.0 5.8 reshape.368
  618.1 4.6 convert_element_type.335
  622.8 4.0 convolution_convert_fusion.6
  629.1 4.3 convolution_convert_fusion.5
  638.9 9.3 %copy.241 = f32[640,4,768]{0,2,1:T(8,128)} copy(f32[640,4,768]{2,0,1:T(8,128)} %get-tuple-element.155) | data formatting | bytes 15728640 | tf_op jit(solution)/shard_map/dot_general | solution.py:436
  655.9 19.0 %multiply_convert_fusion = (bf16[640,3072]{0,1:T(8,128)(2,1)S(1)}, f32[640,3072]{0,1:T(8,128)S(1)}) fusion(f32[640,4,768]{0,2,1:T(8,128)S(1)} %bitcast.312, f32[3072]{0:T(1024)S(1)} %bitcast.338), kind=kLoop, calls=%fused_computation.20 | loop fusion | flops 129761280 | bytes 19673088 | tf_op jit(solution)/shard_map/convert_element_type | solution.py:510
  674.9 5.5 convolution_convert_fusion
  680.5 5.5 fusion.7
  686.0 9.0 convolution_convert_fusion.1
  695.0 127.4 %reduce_grads.1 = (bf16[1152,768]{1,0:T(8,128)(2,1)}, bf16[384,1024]{1,0:T(8,128)(2,1)}, bf16[768,768]{1,0:T(8,128)(2,1)}, bf16[768,768]{1,0:T(8,128)(2,1)}) custom-call(bf16[4,1152,768]{2,1,0:T(8,128)(2,1)} %constant_dynamic-update-slice_fusion.2.refs_0_, bf16[4,384,1024]{2,1,0:T(8,128)(2,1)} %pad_maximum_fusion.refs_1_, bf16[4,768,768]{2,1,0:T(8,128)(2,1)} %bitcast.325, ...), custom_call_target="tpu_custom_call" | custom-call | tf_op jit(solution)/shard_map/reduce_grads/pallas_call | solution.py:321
  844.5 40.2 %psum.7 = f32[7680]{0:T(1024)} all-reduce(f32[7680]{0:T(1024)} %constant_dynamic-update-slice_fusion.9), channel_id=1, replica_groups=mesh['dp'=8,'mp'=4] {'dp','mp'}, use_global_device_ids=true, to_apply=%region_29.30 | all-reduce | flops 7680 | bytes 61440 | tf_op jit(solution)/shard_map/psum | solution.py:564
  (294 shorter events, 198.2 us)
Async XLA Ops:
  7.2 9.6 %copy-start.53 = (bf16[192,768]{1,0:T(8,128)(2,1)S(1)}, bf16[192,768]{1,0:T(8,128)(2,1)}, u32[]{:S(2)}) copy-start(bf16[192,768]{1,0:T(8,128)(2,1)} %param.26) | copy-start | bytes 884740
  7.2 9.7 %copy-start.54 = (bf16[768,192]{0,1:T(8,128)(2,1)S(1)}, bf16[768,192]{0,1:T(8,128)(2,1)}, u32[]{:S(2)}) copy-start(bf16[768,192]{0,1:T(8,128)(2,1)} %param.29) | copy-start | bytes 884740
  7.2 9.7 %copy-start.55 = (bf16[192,768]{1,0:T(8,128)(2,1)S(1)}, bf16[192,768]{1,0:T(8,128)(2,1)}, u32[]{:S(2)}) copy-start(bf16[192,768]{1,0:T(8,128)(2,1)} %param.31) | copy-start | bytes 884740
  7.2 892.8 %reduce-scatter.2.cloned.1.call-start = ((), (), s32[]{:S(2)}) async-start(), calls=%async_computation.1 | async-start | bytes 5939200 | tf_op jit(solution)/shard_map/reduce_scatter | solution.py:545
  18.4 92.4 %copy-start.70 = (bf16[16,40,768]{2,1,0:T(8,128)(2,1)S(1)}, bf16[16,40,768]{2,1,0:T(8,128)(2,1)}, u32[]{:S(2)}) copy-start(bf16[16,40,768]{2,1,0:T(8,128)(2,1)} %param.20) | copy-start | bytes 2949124
  110.8 6.7 copy-start.68
  138.4 6.0 copy-start.11
  140.9 3.5 copy-start.35
  172.0 10.6 %copy-start.50 = (bf16[640,4,192]{0,2,1:T(8,128)(2,1)S(1)}, bf16[640,4,192]{0,2,1:T(8,128)(2,1)}, u32[]{:S(2)}) copy-start(bf16[640,4,192]{0,2,1:T(8,128)(2,1)} %fusion.69) | copy-start | bytes 2949124
  182.6 10.5 %copy-start.5 = (bf16[16,40,12,64]{3,1,2,0:T(8,128)(2,1)}, bf16[16,40,12,64]{3,1,2,0:T(8,128)(2,1)S(1)}, u32[]{:S(2)}) copy-start(bf16[16,40,12,64]{3,1,2,0:T(8,128)(2,1)S(1)} %copy.190) | copy-start | bytes 2949124
  182.6 10.3 %copy-start.75 = (s32[64]{0:T(128)S(1)}, s32[64]{0:T(128)}, u32[]{:S(2)}) copy-start(s32[64]{0:T(128)} %param.23) | copy-start | bytes 772
  210.3 4.3 copy-start.65
  210.4 4.3 copy-start.71
  238.6 18.7 %slice-start.4 = ((s8[6291456]{0:T(1024)(128)(4,1)}), s8[2097152]{0:T(1024)(128)(4,1)S(1)}, s32[]{:S(2)}) async-start(s8[6291456]{0:T(1024)(128)(4,1)} %bitcast.320), calls=%async_computation.6 | async-start | bytes 4194304
  248.7 8.6 slice-start.5
  254.0 3.2 copy-start
  270.4 3.9 copy-start.66
  270.4 3.9 copy-start.73
  273.9 25.4 %copy-start.26 = (f32[640,768]{1,0:T(8,128)}, f32[640,768]{1,0:T(8,128)S(1)}, u32[]{:S(2)}) copy-start(f32[640,768]{1,0:T(8,128)S(1)} %get-tuple-element.151) | copy-start | bytes 5898244
  273.9 56.9 %copy-start.59 = (f32[640]{0:T(1024)}, f32[640]{0:T(1024)S(1)}, u32[]{:S(2)}) copy-start(f32[640]{0:T(1024)S(1)} %broadcast_multiply_fusion.8) | copy-start | bytes 7684
  274.3 56.5 %copy-start.63 = (f32[640]{0:T(1024)}, f32[640]{0:T(1024)S(1)}, u32[]{:S(2)}) copy-start(f32[640]{0:T(1024)S(1)} %add_rsqrt_fusion.1) | copy-start | bytes 7684
  281.9 17.4 %copy-start.4 = (f32[640,4,768]{2,0,1:T(8,128)}, f32[640,4,768]{2,0,1:T(8,128)S(1)}, u32[]{:S(2)}) copy-start(f32[640,4,768]{2,0,1:T(8,128)S(1)} %get-tuple-element.152) | copy-start | bytes 23592964
  299.3 8.7 copy-start.25
  299.3 9.1 copy-start.22
  299.3 9.1 copy-start.61
  310.9 15.7 %slice-start.6 = ((s8[4718592]{0:T(1024)(128)(4,1)}), s8[4194304]{0:T(1024)(128)(4,1)S(1)}, s32[]{:S(2)}) async-start(s8[4718592]{0:T(1024)(128)(4,1)} %bitcast.345), calls=%async_computation.8 | async-start | bytes 8388608
  312.6 14.0 %copy-start.37 = (f32[640,768]{1,0:T(8,128)}, f32[640,768]{1,0:T(8,128)S(1)}, u32[]{:S(2)}) copy-start(f32[640,768]{1,0:T(8,128)S(1)} %get-tuple-element.127) | copy-start | bytes 5898244
  312.6 14.0 %copy-start.27 = (f32[640,768]{1,0:T(8,128)S(1)}, f32[640,768]{1,0:T(8,128)}, u32[]{:S(2)}) copy-start(f32[640,768]{1,0:T(8,128)} %copy-done.26) | copy-start | bytes 5898244
  312.6 14.0 %slice-start.7 = ((s8[4718592]{0:T(1024)(128)(4,1)}), s8[524288]{0:T(1024)(128)(4,1)S(1)}, s32[]{:S(2)}) async-start(s8[4718592]{0:T(1024)(128)(4,1)} %bitcast.345), calls=%async_computation.9 | async-start | bytes 1048576
  359.9 6.0 copy-start.8
  365.9 6.3 copy-start.3
  390.8 11.8 %copy-start.18 = (bf16[10,145,768]{2,1,0:T(8,128)(2,1)}, bf16[10,145,768]{2,1,0:T(8,128)(2,1)S(1)}, u32[]{:S(2)}) copy-start(bf16[10,145,768]{2,1,0:T(8,128)(2,1)S(1)} %copy.291) | copy-start | bytes 6681604
  421.0 4.3 copy-start.20
  486.3 5.8 copy-start.43
  486.3 5.8 copy-start.52
  500.6 4.8 copy-start.29
  520.5 5.0 copy-start.2
  556.9 3.8 copy-start.30
  560.7 4.1 copy-start.32
  562.8 4.1 copy-start.12
  562.8 4.1 copy-start.21
  566.9 3.8 copy-start.19
  583.8 5.8 copy-start.10
  594.0 5.8 copy-start.17
  602.1 3.9 copy-start.16
  608.4 3.8 copy-start.15
  618.1 8.6 copy-start.14
  622.8 6.4 copy-start.72
  629.1 4.3 copy-start.13
  638.9 9.3 %copy-start.44 = (bf16[768,768]{1,0:T(8,128)(2,1)S(1)}, bf16[768,768]{1,0:T(8,128)(2,1)}, u32[]{:S(2)}) copy-start(bf16[768,768]{1,0:T(8,128)(2,1)} %bitcast_convert_fusion.3) | copy-start | bytes 3538948
  638.9 10.4 %copy-start.45 = (bf16[768,768]{1,0:T(8,128)(2,1)S(1)}, bf16[768,768]{1,0:T(8,128)(2,1)}, u32[]{:S(2)}) copy-start(bf16[768,768]{1,0:T(8,128)(2,1)} %bitcast_convert_fusion.2) | copy-start | bytes 3538948
  648.2 3.4 copy-start.47
  649.3 6.6 slice-start
  650.4 3.4 copy-start.40
  650.4 3.4 copy-start.41
  652.7 3.2 copy-start.57
  655.9 19.0 %copy-start.38 = (f32[640,768]{1,0:T(8,128)S(1)}, f32[640,768]{1,0:T(8,128)}, u32[]{:S(2)}) copy-start(f32[640,768]{1,0:T(8,128)} %copy-done.37) | copy-start | bytes 5898244
  655.9 24.5 %slice-start.2 = ((s8[7864320]{0:T(1024)(128)(4,1)}), s8[4194304]{0:T(1024)(128)(4,1)S(1)}, s32[]{:S(2)}) async-start(s8[7864320]{0:T(1024)(128)(4,1)} %bitcast.317), calls=%async_computation.4 | async-start | bytes 8388608
  674.9 5.5 slice-start.3
  680.4 5.6 copy-start.60
  680.4 5.6 copy-start.64
  680.4 5.6 copy-start.67
  680.4 5.6 copy-start.74
  830.2 13.0 %copy-start.62 = (f32[768]{0:T(1024)S(1)}, f32[768]{0:T(1024)}, u32[]{:S(2)}) copy-start(f32[768]{0:T(1024)} %get-tuple-element.115) | copy-start | bytes 9220
  (21 other events, 44.1 us)
Sparse Core Ops, SparseCore 0:
  486.4 86.1 reduce-scatter.1

commit v2 on v0

v2 whole, which is shorter than its diff:
```python
import functools

import jax
import jax.numpy as jnp
from jax import lax
from jax.experimental import pallas as pl
from jax.experimental.pallas import tpu as pltpu
from jax.sharding import PartitionSpec as P

HEAD_DIM = 64
ROWS_MAX = 7
MESH = pl.DeviceIdType.MESH


def place():
    index = lax.axis_index("dp")
    plane = lax.axis_index("mp")
    y, x, c = index // 4, (index // 2) % 2, index % 2
    return index, plane, y, x, c


def partners(index, plane):
    core = (index + 1 - 2 * (index % 2), plane)
    across = (index + 2 - 4 * ((index // 2) % 2), plane)
    along = (index + 4 - 8 * (index // 4), plane)
    planes = [(index, lax.rem(plane + step, 4)) for step in (1, 2, 3)]
    return core, across, along, planes


def greet(peers):
    barrier = pltpu.get_barrier_semaphore()
    for peer in peers:
        pl.semaphore_signal(barrier, inc=1, device_id=peer, device_id_type=MESH)
    pl.semaphore_wait(barrier, len(peers))


class Sends:
    def __init__(self):
        self.stages, self.all = {}, []

    def start(self, name, k, items):
        copies = []
        for source, target, sends, recvs, peer in items:
            copy = pltpu.make_async_remote_copy(
                src_ref=source, dst_ref=target, send_sem=sends, recv_sem=recvs, device_id=peer, device_id_type=MESH
            )
            copy.start()
            copies.append(copy)
        self.stages[name, k] = copies
        self.all.extend(copies)

    def arrived(self, name, k):
        for copy in self.stages[name, k]:
            copy.wait_recv()

    def close(self):
        for copy in self.all:
            copy.wait_send()


class Gather:
    stages = 4

    def __init__(self, chunks, shards, wholes, sems, window):
        self.chunks, self.shards, self.wholes, self.window = chunks, shards, wholes, window
        self.sems = sems
        self.index, self.plane, self.y, self.x, self.c = place()
        self.core, self.across, self.along, self.planes = partners(self.index, self.plane)
        self.others = [lax.rem(self.plane + step, 4) for step in (1, 2, 3)]
        self.sends = Sends()

    def sizes(self, k):
        which, base, rows = self.chunks[k]
        return which, base, rows // 8, self.shards[which].shape[1] // 2

    def level(self, k):
        which, base, r, w = self.sizes(k)
        _, _, send, recv = self.sems[:4]
        items = []
        for h, first in enumerate((self.x * 2 + self.y, self.y * 2 + self.x)):
            here = (pl.ds(pl.multiple_of(base + (self.c * 4 + first) * r, 16), r), pl.ds(h * w, w))
            for j, peer in enumerate(self.planes):
                target = self.wholes[which].at[(self.plane,) + here]
                items.append((self.shards[which].at[here], target, send.at[k, h, j], recv.at[k, h, j], peer))
        self.sends.start("level", k, items)

    def near(self, k):
        which, base, r, w = self.sizes(k)
        send, recv = self.sems[4:6]
        self.sends.arrived("level", k)
        if k + self.window < len(self.chunks):
            self.level(k + self.window)
        items = []
        for h, first in enumerate((self.x * 2 + self.y, self.y * 2 + self.x)):
            row = pl.multiple_of(base + (self.c * 4 + first) * r, 16)
            for j, other in enumerate(self.others):
                piece = self.wholes[which].at[other, pl.ds(row, r), pl.ds(h * w, w)]
                items.append((piece, piece, send.at[k, h, j], recv.at[k, h, j], (self.along, self.across)[h]))
        self.sends.start("near", k, items)

    def far(self, k):
        which, base, r, w = self.sizes(k)
        send, recv = self.sems[6:8]
        self.sends.arrived("near", k)
        items = []
        for h, first in enumerate((self.x, self.y)):
            row = pl.multiple_of(base + (self.c * 4 + first * 2) * r, 16)
            for j, other in enumerate(self.others):
                piece = self.wholes[which].at[other, pl.ds(row, 2 * r), pl.ds(h * w, w)]
                items.append((piece, piece, send.at[k, h, j], recv.at[k, h, j], (self.across, self.along)[h]))
        self.sends.start("far", k, items)

    def cross(self, k):
        which, base, r, w = self.sizes(k)
        send, recv = self.sems[8:10]
        self.sends.arrived("far", k)
        row = pl.multiple_of(base + self.c * 4 * r, 16)
        items = []
        for j, other in enumerate(self.others):
            piece = self.wholes[which].at[other, pl.ds(row, 4 * r), :]
            items.append((piece, piece, send.at[k, j], recv.at[k, j], self.core))
        self.sends.start("core", k, items)

    def begin(self):
        greet([self.core, self.across, self.along] + self.planes)
        for k in range(self.window):
            self.level(k)
        local_sem = self.sems[0]
        self.local = []
        for which, shard in enumerate(self.shards):
            copy = pltpu.make_async_copy(shard, self.wholes[which].at[self.plane], local_sem.at[which])
            copy.start()
            self.local.append(copy)

    def step(self, t):
        if 0 <= t - 4 < len(self.chunks):
            self.cross(t - 4)
        if 0 <= t - 2 < len(self.chunks):
            self.far(t - 2)
        if 0 <= t < len(self.chunks):
            self.near(t)

    @property
    def steps(self):
        return len(self.chunks) + 4

    def ready(self, k):
        self.sends.arrived("core", k)

    @staticmethod
    def scratch(count, total):
        dma = pltpu.SemaphoreType.DMA
        return [dma((count,)), dma((count,))] + [dma((total, 2, 3))] * 6 + [dma((total, 3))] * 2


def gather_kernel(chunks, count, *refs):
    shards, bias, outs, biases = refs[:count], refs[count], refs[count + 1 : 2 * count + 1], refs[2 * count + 1]
    rest = refs[2 * count + 2 :]
    wholes, bias_send, bias_recv, sems = rest[:count], rest[count], rest[count + 1], rest[count + 2 :]
    gather = Gather(chunks, shards, wholes, sems, 3)
    gather.begin()
    gather.sends.start(
        "bias", 0, [(bias, biases.at[gather.plane], bias_send.at[j], bias_recv.at[j], peer) for j, peer in enumerate(gather.planes)]
    )
    biases[gather.plane] = bias[...]
    final = []
    for t in range(gather.steps + 2):
        if 0 <= t - 6 < len(chunks):
            gather.ready(t - 6)
            which = chunks[t - 6][0]
            if t - 5 == len(chunks) or chunks[t - 5][0] != which:
                gather.local[which].wait()
                copy = pltpu.make_async_copy(wholes[which], outs[which], sems[1].at[which])
                copy.start()
                final.append(copy)
        gather.step(t)
    gather.sends.arrived("bias", 0)
    gather.sends.close()
    for copy in final:
        copy.wait()


def gather_weights(shards, bias, chunks):
    count, dma = len(shards), pltpu.SemaphoreType.DMA
    any_space, vmem = pl.BlockSpec(memory_space=pl.ANY), pl.BlockSpec(memory_space=pltpu.VMEM)
    *wholes, biases = pl.pallas_call(
        functools.partial(gather_kernel, chunks, count),
        out_shape=[jax.ShapeDtypeStruct((4,) + s.shape, s.dtype) for s in shards + [bias]],
        in_specs=[any_space] * count + [vmem],
        out_specs=[any_space] * count + [vmem],
        scratch_shapes=[pltpu.VMEM((4,) + s.shape, s.dtype) for s in shards]
        + [dma((3,)), dma((3,))]
        + Gather.scratch(count, len(chunks)),
        compiler_params=pltpu.CompilerParams(collective_id=0, has_side_effects=True, vmem_limit_bytes=62 << 20),
        name="gather_weights",
    )(*shards, bias)
    return wholes, biases


class Reduce:
    def __init__(self, chunks, grads, sums, buffers, sems):
        self.chunks, self.grads, self.sums, self.sems = chunks, grads, sums, sems
        total = len(chunks)
        self.mine, self.core_in, self.near_in, self.far_in, self.plane_in, self.done = (
            buffers[i * total : (i + 1) * total] for i in range(6)
        )
        self.index, self.plane, self.y, self.x, self.c = place()
        self.core, self.across, self.along, self.planes = partners(self.index, self.plane)
        self.others = [lax.rem(self.plane + step, 4) for step in (1, 2, 3)]
        self.sends = Sends()
        self.local, self.final = {}, []
        self.order = [self.begin, self.near, self.far, self.level, self.out_near, self.out_far, self.out_core, self.end]

    @staticmethod
    def scratch(sizes):
        low, dma, total = jnp.bfloat16, pltpu.SemaphoreType.DMA, len(sizes)
        shapes = [[(4, r // 2, w) for r, w in sizes]] * 2
        shapes += [[(2, 4, r // 4, w // 2) for r, w in sizes], [(2, 4, r // 8, w // 2) for r, w in sizes]]
        shapes += [[(2, 3, r // 8, w // 2) for r, w in sizes], [(r, w) for r, w in sizes]]
        buffers = [pltpu.VMEM(shape, low) for group in shapes for shape in group]
        sems = [dma((total,))] * 4 + [dma((total, 2))] * 8 + [dma((total, 2, 3))] * 2 + [dma((total,))] * 2
        return buffers, sems

    def sizes(self, k):
        which, base, rows = self.chunks[k]
        return which, base, rows // 8, self.grads[which].shape[2] // 2

    @staticmethod
    def add(total, total_row, total_col, part, part_col, rows, cols):
        @pl.loop(0, rows // 16)
        def _(i):
            for shard in range(4):
                here = (shard, pl.ds(pl.multiple_of(total_row + i * 16, 16), 16), pl.ds(total_col, cols))
                there = (shard, pl.ds(pl.multiple_of(i * 16, 16), 16), pl.ds(part_col, cols))
                total[here] = (total[here].astype(jnp.float32) + part[there].astype(jnp.float32)).astype(jnp.bfloat16)

    def places(self, r, w):
        return [((self.x * 2 + self.y) * r, 0), ((self.y * 2 + self.x) * r, w)]

    def begin(self, k):
        which, base, r, w = self.sizes(k)
        theirs = pl.multiple_of(base + (1 - self.c) * 4 * r, 16)
        ours = pl.multiple_of(base + self.c * 4 * r, 16)
        source = self.grads[which].at[:, pl.ds(theirs, 4 * r), :]
        self.sends.start("core", k, [(source, self.core_in[k], self.sems[0].at[k], self.sems[1].at[k], self.core)])
        self.local[k] = pltpu.make_async_copy(
            self.grads[which].at[:, pl.ds(ours, 4 * r), :], self.mine[k], self.sems[2].at[k]
        )
        self.local[k].start()

    def near(self, k):
        which, base, r, w = self.sizes(k)
        self.local[k].wait()
        self.sends.arrived("core", k)
        self.add(self.mine[k], 0, 0, self.core_in[k], 0, 4 * r, 2 * w)
        items = []
        for h, (bit, peer) in enumerate([(self.x, self.across), (self.y, self.along)]):
            row = pl.multiple_of((1 - bit) * 2 * r, 16)
            source = self.mine[k].at[:, pl.ds(row, 2 * r), pl.ds(h * w, w)]
            items.append((source, self.near_in[k].at[h], self.sems[4].at[k, h], self.sems[5].at[k, h], peer))
        self.sends.start("near", k, items)

    def far(self, k):
        which, base, r, w = self.sizes(k)
        self.sends.arrived("near", k)
        items = []
        for h, (bit, second, peer) in enumerate([(self.x, self.y, self.along), (self.y, self.x, self.across)]):
            row = bit * 2 * r
            self.add(self.mine[k], row, h * w, self.near_in[k].at[h], 0, 2 * r, w)
            row = pl.multiple_of(row + (1 - second) * r, 16)
            source = self.mine[k].at[:, pl.ds(row, r), pl.ds(h * w, w)]
            items.append((source, self.far_in[k].at[h], self.sems[6].at[k, h], self.sems[7].at[k, h], peer))
        self.sends.start("far", k, items)

    def level(self, k):
        which, base, r, w = self.sizes(k)
        self.sends.arrived("far", k)
        items = []
        for h, (row, col) in enumerate(self.places(r, w)):
            self.add(self.mine[k], row, col, self.far_in[k].at[h], 0, r, w)
            row = pl.multiple_of(row, 16)
            for j in range(3):
                source = self.mine[k].at[self.others[j], pl.ds(row, r), pl.ds(col, w)]
                items.append(
                    (source, self.plane_in[k].at[h, j], self.sems[12].at[k, h, j], self.sems[13].at[k, h, j], self.planes[j])
                )
        self.sends.start("level", k, items)

    def out_near(self, k):
        which, base, r, w = self.sizes(k)
        self.sends.arrived("level", k)
        items = []
        for h, (row, col) in enumerate(self.places(r, w)):

            @pl.loop(0, r // 16)
            def _(i):
                step = pl.ds(pl.multiple_of(i * 16, 16), 16)
                here = pl.ds(pl.multiple_of(row + i * 16, 16), 16)
                total = self.mine[k][self.plane, here, pl.ds(col, w)].astype(jnp.float32)
                for j in range(3):
                    total = total + self.plane_in[k][h, j, step, :].astype(jnp.float32)
                here = pl.ds(pl.multiple_of(self.c * 4 * r + row + i * 16, 16), 16)
                self.done[k][here, pl.ds(col, w)] = total.astype(jnp.bfloat16)

            piece = self.done[k].at[pl.ds(pl.multiple_of(self.c * 4 * r + row, 16), r), pl.ds(col, w)]
            peer = (self.along, self.across)[h]
            items.append((piece, piece, self.sems[8].at[k, h], self.sems[9].at[k, h], peer))
        self.sends.start("out_near", k, items)

    def out_far(self, k):
        which, base, r, w = self.sizes(k)
        self.sends.arrived("out_near", k)
        items = []
        for h, (bit, peer) in enumerate([(self.x, self.across), (self.y, self.along)]):
            row = pl.multiple_of((self.c * 4 + bit * 2) * r, 16)
            piece = self.done[k].at[pl.ds(row, 2 * r), pl.ds(h * w, w)]
            items.append((piece, piece, self.sems[10].at[k, h], self.sems[11].at[k, h], peer))
        self.sends.start("out_far", k, items)

    def out_core(self, k):
        which, base, r, w = self.sizes(k)
        self.sends.arrived("out_far", k)
        piece = self.done[k].at[pl.ds(pl.multiple_of(self.c * 4 * r, 16), 4 * r), :]
        self.sends.start("out_core", k, [(piece, piece, self.sems[14].at[k], self.sems[15].at[k], self.core)])

    def end(self, k):
        which, base, r, w = self.sizes(k)
        self.sends.arrived("out_core", k)
        copy = pltpu.make_async_copy(self.done[k], self.sums[which].at[pl.ds(base, 8 * r), :], self.sems[3].at[k])
        copy.start()
        self.final.append(copy)

    @property
    def steps(self):
        return len(self.chunks) + len(self.order) - 1

    def step(self, t):
        for s in reversed(range(len(self.order))):
            if 0 <= t - s < len(self.chunks):
                self.order[s](t - s)

    def close(self):
        self.sends.close()
        for copy in self.final:
            copy.wait()


def reduce_kernel(chunks, count, *refs):
    grads, patch, vectors = refs[:count], refs[count], refs[count + 1]
    sums, windows, vector_sum = refs[count + 2 : 2 * count + 2], refs[2 * count + 2], refs[2 * count + 3]
    rest = refs[2 * count + 4 :]
    total = 6 * len(chunks)
    buffers, sems = rest[:total], rest[total : total + 16]
    vector_in, patch_send, patch_recv, vector_send, vector_recv, patch_local = rest[total + 16 :]
    reduce = Reduce(chunks, grads, sums, buffers, sems)
    greet([reduce.core, reduce.across, reduce.along] + reduce.planes)
    reduce.sends.start(
        "patch",
        0,
        [
            (patch.at[other], windows.at[reduce.plane], patch_send.at[j], patch_recv.at[j], peer)
            for j, (other, peer) in enumerate(zip(reduce.others, reduce.planes))
        ],
    )
    copy = pltpu.make_async_copy(patch.at[reduce.plane], windows.at[reduce.plane], patch_local)
    copy.start()
    vector_sum[0] = vectors[...]
    for t in range(reduce.steps):
        if t < 3:
            peer = (reduce.core, reduce.across, reduce.along)[t]
            reduce.sends.start("vector", t, [(vector_sum.at[t], vector_in.at[t], vector_send.at[t], vector_recv.at[t], peer)])
        if t == 3:
            reduce.sends.start(
                "vector",
                t,
                [
                    (vector_sum.at[3], vector_in.at[3 + j], vector_send.at[3 + j], vector_recv.at[3 + j], peer)
                    for j, peer in enumerate(reduce.planes)
                ],
            )
        reduce.step(t)
        if t < 3:
            reduce.sends.arrived("vector", t)
            vector_sum[t + 1] = vector_sum[t] + vector_in[t]
        if t == 3:
            reduce.sends.arrived("vector", t)
            vector_sum[4] = vector_sum[3] + ((vector_in[3] + vector_in[4]) + vector_in[5])
    reduce.sends.arrived("patch", 0)
    reduce.close()
    copy.wait()


def reduce_grads(grads, patch, vectors, chunks):
    count, dma = len(grads), pltpu.SemaphoreType.DMA
    any_space, vmem = pl.BlockSpec(memory_space=pl.ANY), pl.BlockSpec(memory_space=pltpu.VMEM)
    buffers, sems = Reduce.scratch([(rows, grads[which].shape[2]) for which, _, rows in chunks])
    *sums, windows, vector_sum = pl.pallas_call(
        functools.partial(reduce_kernel, chunks, count),
        out_shape=[jax.ShapeDtypeStruct(g.shape[1:], g.dtype) for g in grads]
        + [jax.ShapeDtypeStruct(patch.shape, patch.dtype), jax.ShapeDtypeStruct((5,) + vectors.shape, vectors.dtype)],
        in_specs=[any_space] * (count + 1) + [vmem],
        out_specs=[any_space] * (count + 1) + [vmem],
        scratch_shapes=buffers
        + sems
        + [pltpu.VMEM((6,) + vectors.shape, vectors.dtype), dma((3,)), dma((3,)), dma((6,)), dma((6,)), dma(())],
        compiler_params=pltpu.CompilerParams(collective_id=1, has_side_effects=True, vmem_limit_bytes=62 << 20),
        name="reduce_grads",
    )(*grads, patch, vectors)
    return sums, windows, vector_sum[4]


def nn(left, right):
    return lax.dot_general(left, right, (((1,), (0,)), ((), ())), preferred_element_type=jnp.float32)


def nt(left, right):
    return lax.dot_general(left, right, (((1,), (1,)), ((), ())), preferred_element_type=jnp.float32)


def tn(left, right):
    return lax.dot_general(left, right, (((0,), (0,)), ((), ())), preferred_element_type=jnp.float32)


def part(ref, which):
    inner = ref.shape[2] // 4 if ref.shape[2] == 768 else 192
    return jnp.concatenate([ref[m, which * 192 : (which + 1) * 192, :] for m in range(4)], axis=0)


def store_part(ref, which, value):
    low = value.astype(jnp.bfloat16)
    for m in range(4):
        ref[m, which * 192 : (which + 1) * 192, :] = low[m * 192 : (m + 1) * 192]


def tiles(amount, step):
    def wrap(body):
        @pl.loop(0, amount // step)
        def _(i):
            body(pl.ds(pl.multiple_of(i * step, step), step))

    return wrap


def lanes():
    place = lax.broadcasted_iota(jnp.int32, (1, 2 * HEAD_DIM), 1)
    low = place < HEAD_DIM
    return low, low.astype(jnp.float32), 1.0 - low.astype(jnp.float32)


def norm_forward(total, unit, inverse, value, value_low, gain, shift):
    @tiles(total.shape[0], 80)
    def _(rows):
        hidden = total[rows, :]
        center = hidden - jnp.mean(hidden, axis=-1, keepdims=True)
        factor = lax.rsqrt(jnp.mean(center * center, axis=-1, keepdims=True) + 1e-06)
        scaled = center * factor
        result = scaled * gain[...] + shift[...]
        if unit is not None:
            unit[rows, :] = scaled
            inverse[rows, :] = jnp.broadcast_to(factor, (80, 128))
        if value is not None:
            value[rows, :] = result
        value_low[rows, :] = result.astype(jnp.bfloat16)


def norm_reverse(upstream, unit, inverse, gain, gain_grad, shift_grad, grad, grad_low):
    gain_grad[...] = jnp.zeros_like(gain_grad)
    shift_grad[...] = jnp.zeros_like(shift_grad)

    @tiles(upstream.shape[0], 80)
    def _(rows):
        up = upstream[rows, :].astype(jnp.float32)
        scaled = unit[rows, :]
        factor = inverse[rows, :][:, :1]
        gain_grad[...] += jnp.sum(up * scaled, axis=0, keepdims=True)
        shift_grad[...] += jnp.sum(up, axis=0, keepdims=True)
        inner = up * gain[...]
        result = factor * (
            inner
            - jnp.mean(inner, axis=-1, keepdims=True)
            - scaled * jnp.mean(inner * scaled, axis=-1, keepdims=True)
        )
        grad[rows, :] = result
        grad_low[rows, :] = result.astype(jnp.bfloat16)


def softmax(scores):
    raised = jnp.exp(scores - jnp.max(scores, axis=-1, keepdims=True))
    return (raised * (1.0 / jnp.sum(raised, axis=-1, keepdims=True))).astype(jnp.bfloat16)


def attend_self(queries, keys, values, pair_ok, probs, context):
    low, first, second = lanes()
    first_low, second_low = first.astype(jnp.bfloat16), second.astype(jnp.bfloat16)

    @pl.loop(0, pair_ok.shape[0])
    def _(pair):
        rows = pl.ds(pl.multiple_of(pair * 80, 80), 80)
        allowed = pair_ok[pair] > 0
        allowed = jnp.concatenate([allowed, allowed], axis=0)
        for tile in range(6):
            cols = slice(tile * 128, (tile + 1) * 128)
            query = queries[rows, cols]
            both = jnp.concatenate([query * first_low, query * second_low], axis=0)
            scores = jnp.where(allowed, nt(both, keys[rows, cols]) * HEAD_DIM ** (-0.5), -1000000000.0)
            weights = softmax(scores)
            probs[pair, tile] = weights
            mixed = nn(weights, values[rows, cols])
            context[rows, cols] = jnp.where(low, mixed[:80], mixed[80:]).astype(jnp.bfloat16)


def attend_cross(image, wide, keys, values, cell_ok, probs):
    low, first, second = lanes()

    @pl.loop(0, cell_ok.shape[0])
    def _(row):
        rows = pl.ds(pl.multiple_of(row * 40, 40), 40)
        which = image[row]
        allowed = jnp.broadcast_to(cell_ok[pl.ds(row, 1), :], (80, cell_ok.shape[1])) > 0
        for tile in range(6):
            cols = slice(tile * 128, (tile + 1) * 128)
            query = wide[rows, cols]
            both = jnp.concatenate([query * first, query * second], axis=0).astype(jnp.bfloat16)
            scores = jnp.where(allowed, nt(both, keys[which, :, cols]) * HEAD_DIM ** (-0.5), -1000000000.0)
            weights = softmax(scores)
            probs[row, tile] = weights
            mixed = nn(weights, values[which, :, cols])
            wide[rows, cols] = jnp.where(low, mixed[:40], mixed[40:])


def forward_kernel(
    image, tokens, near, pair_ok, cell_ok, self_weights, cross_weights, keyval, first_gain, first_shift, second_gain,
    second_shift,
    queries, keys, values, self_probs, self_context, first_unit, first_inverse, first_low, cross_queries, image_keys,
    image_values, cross_probs, cross_context, second_unit, second_inverse, second_value, second_low,
    total, first_value, wide,
):
    bf16 = jnp.bfloat16
    for target, which in ((queries, 0), (keys, 1), (values, 2)):
        target[...] = nt(tokens[...], part(self_weights, which)).astype(bf16)
    attend_self(queries, keys, values, pair_ok, self_probs, self_context)
    total[...] = nn(self_context[...], part(self_weights, 3)) + tokens[...].astype(jnp.float32)
    norm_forward(total, first_unit, first_inverse, first_value, first_low, first_gain, first_shift)
    cross_queries[...] = nt(first_low[...], part(cross_weights, 0)).astype(bf16)
    wide[...] = cross_queries[...].astype(jnp.float32)
    images, cells, depth = near.shape
    half = images // 2
    for target, which in ((image_keys, 0), (image_values, 1)):
        weight = part(keyval, which)
        for step in range(2):
            block = near[step * half : (step + 1) * half].reshape(half * cells, depth)
            target[step * half : (step + 1) * half] = nt(block, weight).astype(bf16).reshape(half, cells, -1)
    attend_cross(image, wide, image_keys, image_values, cell_ok, cross_probs)
    cross_context[...] = wide[...].astype(bf16)
    total[...] = nn(cross_context[...], part(cross_weights, 1)) + first_value[...]
    norm_forward(total, second_unit, second_inverse, second_value, second_low, second_gain, second_shift)


def feed_kernel(
    second_value, second_low, expand, shrink, bias, gain, shift, cotangent,
    joined, expand_grad, shrink_grad, bias_grad, gain_grad, shift_grad, second_up,
    active, slope, wide, unit, inverse, feed_low,
):
    bf16 = jnp.bfloat16
    second_up[...] = second_value[...]

    @pl.loop(0, 4)
    def _(m):
        wide[...] = nt(second_low[...], expand[m])

        @tiles(wide.shape[0], 40)
        def _(rows):
            inner = wide[rows, :] + bias[pl.ds(m, 1), :]
            share = 0.5 * (1.0 + lax.erf(inner * 0.5**0.5))
            wide[rows, :] = inner * share
            unit[rows, :] = share + inner * (jnp.exp(-0.5 * inner * inner) * 0.3989422804014327)

        active[m] = wide[...].astype(bf16)
        slope[m] = unit[...].astype(bf16)
        second_up[...] += nn(active[m], shrink[m])

    norm_forward(second_up, unit, inverse, None, joined, gain, shift)
    norm_reverse(cotangent, unit, inverse, gain, gain_grad, shift_grad, second_up, feed_low)

    @pl.loop(0, 4)
    def _(m):
        shrink_grad[m] = tn(active[m], feed_low[...]).astype(bf16)
        wide[...] = nt(feed_low[...], shrink[m])
        bias_grad[pl.ds(m, 1), :] = jnp.zeros((1, 768), jnp.float32)

        @tiles(wide.shape[0], 80)
        def _(rows):
            low = (wide[rows, :] * slope[m, rows, :].astype(jnp.float32)).astype(bf16)
            active[m, rows, :] = low
            bias_grad[pl.ds(m, 1), :] += jnp.sum(low.astype(jnp.float32), axis=0, keepdims=True)

        expand_grad[m] = tn(active[m], second_low[...]).astype(bf16)
        second_up[...] += nn(active[m], expand[m])


def cross_back_kernel(
    image, near, cross_weights, keyval, cross_queries, image_keys, image_values, cross_probs, cross_context, second_up,
    second_unit, second_inverse, second_gain, first_low,
    weights_grad, keyval_grad, patch_part, gain_grad, shift_grad, first_up,
    grad_low, wide, turn, key_sum, value_sum, query_low,
):
    bf16 = jnp.bfloat16
    low, first, second = lanes()
    norm_reverse(second_up, second_unit, second_inverse, second_gain, gain_grad, shift_grad, first_up, grad_low)
    store_part(weights_grad, 1, tn(cross_context[...], grad_low[...]))
    wide[...] = nt(grad_low[...], part(cross_weights, 1)).astype(bf16).astype(jnp.float32)
    turn[...] = cross_queries[...].astype(jnp.float32)
    key_sum[...] = jnp.zeros_like(key_sum)
    value_sum[...] = jnp.zeros_like(value_sum)

    @pl.loop(0, cross_probs.shape[0])
    def _(row):
        rows = pl.ds(pl.multiple_of(row * 40, 40), 40)
        which = image[row]
        for tile in range(6):
            cols = slice(tile * 128, (tile + 1) * 128)
            query, grad = turn[rows, cols], wide[rows, cols]
            queries = jnp.concatenate([query * first, query * second], axis=0).astype(bf16)
            grads = jnp.concatenate([grad * first, grad * second], axis=0).astype(bf16)
            weights = cross_probs[row, tile]
            probs = weights.astype(jnp.float32)
            upstream = nt(grads, image_values[which, :, cols])
            back = (probs * (upstream - jnp.sum(probs * upstream, axis=-1, keepdims=True))).astype(bf16)
            mixed = nn(back, image_keys[which, :, cols])
            turn[rows, cols] = jnp.where(low, mixed[:40], mixed[40:]) * HEAD_DIM ** (-0.5)
            key_sum[which, :, cols] += tn(back, queries) * HEAD_DIM ** (-0.5)
            value_sum[which, :, cols] += tn(weights, grads)

    query_low[...] = turn[...].astype(bf16)
    store_part(weights_grad, 0, tn(query_low[...], first_low[...]))
    first_up[...] += nn(query_low[...], part(cross_weights, 0))
    images, cells, depth = near.shape
    amount = images * cells
    for source, which in ((key_sum, 0), (value_sum, 1)):
        flat = source[...].astype(bf16).reshape(amount, -1)
        store_part(keyval_grad, which, tn(flat, near[...].reshape(amount, depth)))
    for step in range(2):
        here = slice(step * (images // 2), (step + 1) * (images // 2))
        block = nn(key_sum[here].astype(bf16).reshape(amount // 2, -1), part(keyval, 0))
        block += nn(value_sum[here].astype(bf16).reshape(amount // 2, -1), part(keyval, 1))
        block = block.astype(bf16)
        for m in range(4):
            patch_part[m, here] = block[:, m * 256 : (m + 1) * 256].reshape(images // 2, cells, 256)


def self_back_kernel(
    tokens, self_weights, queries, keys, values, self_probs, self_context, first_up, first_unit, first_inverse,
    first_gain,
    weights_grad, gain_grad, shift_grad, text_grad,
    grad_low, context_low, query_low, key_low, value_low,
):
    bf16 = jnp.bfloat16
    low, first, second = lanes()
    first_mask, second_mask = first.astype(bf16), second.astype(bf16)
    norm_reverse(first_up, first_unit, first_inverse, first_gain, gain_grad, shift_grad, text_grad, grad_low)
    store_part(weights_grad, 3, tn(self_context[...], grad_low[...]))
    context_low[...] = nt(grad_low[...], part(self_weights, 3)).astype(bf16)

    @pl.loop(0, self_probs.shape[0])
    def _(pair):
        rows = pl.ds(pl.multiple_of(pair * 80, 80), 80)
        for tile in range(6):
            cols = slice(tile * 128, (tile + 1) * 128)
            query, grad = queries[rows, cols], context_low[rows, cols]
            both = jnp.concatenate([query * first_mask, query * second_mask], axis=0)
            grads = jnp.concatenate([grad * first_mask, grad * second_mask], axis=0)
            weights = self_probs[pair, tile]
            probs = weights.astype(jnp.float32)
            upstream = nt(grads, values[rows, cols])
            back = (probs * (upstream - jnp.sum(probs * upstream, axis=-1, keepdims=True))).astype(bf16)
            mixed = nn(back, keys[rows, cols])
            query_low[rows, cols] = (jnp.where(low, mixed[:80], mixed[80:]) * HEAD_DIM ** (-0.5)).astype(bf16)
            key_low[rows, cols] = (tn(back, both) * HEAD_DIM ** (-0.5)).astype(bf16)
            value_low[rows, cols] = tn(weights, grads).astype(bf16)

    for source, which in ((query_low, 0), (key_low, 1), (value_low, 2)):
        store_part(weights_grad, which, tn(source[...], tokens[...]))
        text_grad[...] += nn(source[...], part(self_weights, which))


def place_kernel(starts, windows, result):
    cells = result.shape[1]
    result[...] = jnp.zeros_like(result)
    for m in range(windows.shape[0]):

        @pl.loop(0, windows.shape[1])
        def _(i):
            result[starts[m] + i] += windows[m, i, :cells, :].astype(jnp.float32)


def on_core(kernel, name, inputs, outputs, scratch, scalars=0):
    vmem, smem = pl.BlockSpec(memory_space=pltpu.VMEM), pl.BlockSpec(memory_space=pltpu.SMEM)
    return pl.pallas_call(
        kernel,
        out_shape=[jax.ShapeDtypeStruct(shape, kind) for shape, kind in outputs],
        in_specs=[smem] * scalars + [vmem] * (len(inputs) - scalars),
        out_specs=[vmem] * len(outputs),
        scratch_shapes=[pltpu.VMEM(shape, kind) for shape, kind in scratch],
        compiler_params=pltpu.CompilerParams(vmem_limit_bytes=62 << 20),
        name=name,
    )(*inputs)


def image_windows(parts, rows, group_images):
    group_rows = parts * rows
    first = [m * rows // ROWS_MAX for m in range(parts)]
    last = [group_images - 1 - max(0, -(-(group_rows - (m + 1) * rows - (ROWS_MAX - 1)) // ROWS_MAX)) for m in range(parts)]
    last = [min(stop, (m + 1) * rows - 1) for m, stop in enumerate(last)]
    window = max(stop - start + 1 for start, stop in zip(first, last))
    return [min(start, group_images - window) for start in first], window


def gather_shards(shards, bias, chunks, own):
    if own:
        return gather_weights(shards, bias, chunks)
    return [lax.all_gather(shard, "mp", axis=0) for shard in shards], lax.all_gather(bias, "mp", axis=0)


def reduce_shards(grads, patch, vectors, chunks, own):
    if own:
        return reduce_grads(grads, patch, vectors, chunks)
    sums = [
        lax.psum(lax.psum_scatter(grad.astype(jnp.float32), "mp", scatter_dimension=0, tiled=True)[0], "dp")
        for grad in grads
    ]
    windows = lax.all_to_all(patch, "mp", split_axis=0, concat_axis=0, tiled=True)
    return sums, windows, lax.psum(vectors, ("dp", "mp"))


def per_device(
    tokens, patches, image_rows, row_lengths, box_mask, self_project, self_output, first_gain, first_shift, cross_query,
    cross_keyval, cross_output, second_gain, second_shift, expand_weight, expand_bias, shrink_weight, third_gain,
    third_shift, cotangent, *, parts, own,
):
    bf16, f32 = jnp.bfloat16, jnp.float32
    rows, slots, width = tokens.shape
    group_images, cells, depth = patches.shape
    starts, window = image_windows(parts, rows, group_images)
    padded = -(-cells // 16) * 16
    plane = lax.axis_index("mp")
    start = jnp.asarray(starts, jnp.int32)[plane]
    amount, pairs, tiles_of = rows * slots, rows // 2, width // 128

    inner, hidden = self_output.shape[0], expand_bias.shape[0]
    shards = [
        jnp.concatenate([self_project[0].T, self_project[1].T, self_project[2].T, self_output], axis=0),
        jnp.concatenate([cross_query.T, cross_output], axis=0),
        jnp.concatenate([cross_keyval[0].T, cross_keyval[1].T], axis=0),
        expand_weight.T,
        shrink_weight,
    ]
    chunks = [(0, 0, 384), (0, 384, 384), (1, 0, 384), (2, 0, 384), (3, 0, 384), (3, 384, 384), (4, 0, 384), (4, 384, 384)]
    bias_rows = jnp.pad(expand_bias.reshape(hidden // 128, 128), ((0, -(hidden // 128) % 8), (0, 0)))
    (self_weights, cross_weights, keyval, expand, shrink), biases = gather_shards(shards, bias_rows, chunks, own)
    bias = biases[:, : hidden // 128].reshape(parts, hidden)

    counts = image_rows[0]
    ends = jnp.cumsum(counts)
    row_index = plane * rows + jnp.arange(rows, dtype=jnp.int32)
    owner = jnp.sum(row_index[:, None] >= ends[None, :], axis=1).astype(jnp.int32)
    caption = jnp.any(row_index[:, None] == (ends - counts)[None, :], axis=1)
    lengths = lax.dynamic_slice_in_dim(row_lengths, plane * rows, rows, 0)
    boxes = lax.dynamic_slice_in_dim(box_mask, plane * rows, rows, 0)
    cell_ok = jnp.pad((caption[:, None] | (boxes > 0)).astype(f32), ((0, 0), (0, padded - cells)))
    slot = jnp.arange(2 * slots, dtype=jnp.int32)
    key_ok = (slot % slots)[None, :] < jnp.repeat(lengths.reshape(pairs, 2), slots, axis=1)
    pair_ok = (key_ok[:, None, :] & ((slot // slots)[:, None] == (slot // slots)[None, :])[None]).astype(f32)
    near = lax.dynamic_slice_in_dim(patches, start, window, 0)
    near = jnp.pad(near, ((0, 0), (0, padded - cells), (0, 0)))
    image = owner - start

    text = tokens.reshape(amount, width)
    row = lambda vector: vector.reshape(1, width)
    flat, unit_row, vector = (amount, width), (amount, 128), ((1, width), f32)
    low_flat, full_flat = (flat, bf16), (flat, f32)
    probs_self, probs_cross = (pairs, tiles_of, 4 * slots, 2 * slots), (rows, tiles_of, 2 * slots, padded)
    image_part = ((window, padded, width), bf16)
    (
        queries, keys, values, self_probs, self_context, first_unit, first_inverse, first_low, cross_queries, image_keys,
        image_values, cross_probs, cross_context, second_unit, second_inverse, second_value, second_low,
    ) = on_core(
        forward_kernel,
        "forward",
        [image, text, near, pair_ok, cell_ok, self_weights, cross_weights, keyval]
        + [row(v) for v in (first_gain, first_shift, second_gain, second_shift)],
        [low_flat] * 3 + [(probs_self, bf16), low_flat, full_flat, (unit_row, f32), low_flat, low_flat]
        + [image_part, image_part, (probs_cross, bf16), low_flat, full_flat, (unit_row, f32), full_flat, low_flat],
        [full_flat] * 3,
        scalars=1,
    )
    joined, expand_grad, shrink_grad, bias_grad, third_gain_grad, third_shift_grad, second_up = on_core(
        feed_kernel,
        "feed",
        [second_value, second_low, expand, shrink, bias, row(third_gain), row(third_shift), cotangent.reshape(flat)],
        [low_flat, (expand.shape, bf16), (shrink.shape, bf16), (bias.shape, f32), vector, vector, full_flat],
        [((parts,) + flat, bf16)] * 2 + [full_flat, full_flat, (unit_row, f32), low_flat],
    )
    cross_weights_grad, keyval_grad, patch, second_gain_grad, second_shift_grad, first_up = on_core(
        cross_back_kernel,
        "cross_back",
        [image, near, cross_weights, keyval, cross_queries, image_keys, image_values, cross_probs, cross_context, second_up]
        + [second_unit, second_inverse, row(second_gain), first_low],
        [(cross_weights.shape, bf16), (keyval.shape, bf16), ((parts, window, padded, depth // parts), bf16)]
        + [vector, vector, full_flat],
        [low_flat, full_flat, full_flat, (image_part[0], f32), (image_part[0], f32), low_flat],
        scalars=1,
    )
    self_weights_grad, first_gain_grad, first_shift_grad, text_grad = on_core(
        self_back_kernel,
        "self_back",
        [text, self_weights, queries, keys, values, self_probs, self_context, first_up, first_unit, first_inverse]
        + [row(first_gain)],
        [(self_weights.shape, bf16), vector, vector, full_flat],
        [low_flat] * 5,
    )
    vectors = jnp.concatenate(
        [bias_grad.reshape(-1)]
        + [
            grad.reshape(-1)
            for grad in (
                first_gain_grad, first_shift_grad, second_gain_grad, second_shift_grad, third_gain_grad, third_shift_grad
            )
        ]
    )
    entries = vectors.shape[0]
    vectors = jnp.pad(vectors.reshape(entries // 128, 128), ((0, -(entries // 128) % 8), (0, 0)))
    grads = [self_weights_grad, cross_weights_grad, keyval_grad, expand_grad, shrink_grad]
    order = [(4, 0, 768), (3, 0, 768), (1, 0, 384), (2, 0, 384), (0, 0, 768)]
    sums, windows, vectors = reduce_shards(grads, patch, vectors, order, own)
    (patch_grad,) = on_core(
        place_kernel, "place", [jnp.asarray(starts, jnp.int32), windows], [((group_images, cells, depth // parts), f32)], [],
        scalars=1,
    )
    self_sum, cross_sum, keyval_sum, expand_sum, shrink_sum = (total.astype(f32) for total in sums)
    vectors = vectors.reshape(-1)
    bias_sum = lax.dynamic_slice_in_dim(vectors, plane * hidden, hidden, 0)
    norms = [vectors[parts * hidden + i * width : parts * hidden + (i + 1) * width] for i in range(6)]
    return (
        joined.reshape(tokens.shape),
        text_grad.reshape(tokens.shape),
        patch_grad,
        jnp.stack([self_sum[c * inner : (c + 1) * inner].T for c in range(3)]),
        self_sum[3 * inner :],
        norms[0],
        norms[1],
        cross_sum[:inner].T,
        jnp.stack([keyval_sum[:inner].T, keyval_sum[inner:].T]),
        cross_sum[inner:],
        norms[2],
        norms[3],
        expand_sum.T,
        bias_sum,
        shrink_sum,
        norms[4],
        norms[5],
    )


def solution(mesh):
    parts = mesh.shape["mp"]
    own = mesh.shape["dp"] == 8 and parts == 4
    return jax.shard_map(
        functools.partial(per_device, parts=parts, own=own),
        mesh=mesh,
        in_specs=(
            P(("dp", "mp"), None, None),
            P("dp", None, None),
            P("dp", None),
            P("dp"),
            P("dp", None),
            P(None, None, "mp"),
            P("mp", None),
            P(),
            P(),
            P(None, "mp"),
            P(None, None, "mp"),
            P("mp", None),
            P(),
            P(),
            P(None, "mp"),
            P("mp"),
            P("mp", None),
            P(),
            P(),
            P(("dp", "mp"), None, None),
        ),
        out_specs=(
            P(("dp", "mp"), None, None),
            P(("dp", "mp"), None, None),
            P("dp", None, "mp"),
            P(None, None, "mp"),
            P("mp", None),
            P(),
            P(),
            P(None, "mp"),
            P(None, None, "mp"),
            P("mp", None),
            P(),
            P(),
            P(None, "mp"),
            P("mp"),
            P("mp", None),
            P(),
            P(),
        ),
        check_vma=False,
    )
```

time: 1650 us -> 513 us (0.31)
  waiting for transfers between devices: 1120 us -> 0 us
  Pallas kernels: 0 us -> 460 us
  matrix products: 225 us -> 0 us
  local copies, waits for them, and re-layouts: 170 us -> 29.1 us
  blocking collectives: 57.1 us -> 0 us
  other arithmetic: 43.3 us -> 15.3 us
    reduce_scatter x7 -> x0, waiting for transfers between devices: 620 us -> none  [the longest x2 269 us: scatter_out(): lax.psum_scatter(jnp.dot(inputs_all, weight, preferred_element_type=jnp.f...]
    pallas_call x0 -> x7, Pallas kernels: none -> 460 us  [the longest x5 207 us: on_core(): pl.pallas_call(kernel, out_shape=[jax.ShapeDtypeStruct(shape, kind) for s...]
    all_gather x6 -> x0, waiting for transfers between devices: 357 us -> none  [the longest x2 121 us: gather_rows(): return lax.all_gather(local_rows, 'mp', axis=0, tiled=True)]
    dot_general x44 -> x0, matrix products: 225 us -> none  [the longest x1 22.8 us: per_device(): jnp.dot(second_all, expand_weight, preferred_element_type=jnp.float32)]
    psum x1 -> x0, waiting for transfers between devices: 147 us -> none  [per_device(): lax.psum((self_project_grad, self_output_grad, cross_query_grad, cross_ke...]
    convert_element_type x20 -> x0, local copies, waits for them, and re-layouts: 88.1 us -> none  [the longest x1 8.81 us: per_device(): row_values = jnp.einsum('gi,ipe->gpe', member_low, image_values, preferre...]
    psum x2 -> x0, blocking collectives: 57.1 us -> none  [the longest x1 42.8 us: per_device(): lax.psum((first_gain_grad, first_shift_grad, second_gain_grad, second_shi...]
    reshape x9 -> x10, local copies, waits for them, and re-layouts: 49.8 us -> 3.74 us  [the longest x6 3.48 us: per_device(): row = lambda vector: vector.reshape(1, width)]
  transfers between devices with their start and end apart: 14 -> 0, of which waited for: 13 -> 0; matrix products, arithmetic and copies ran while one was open for 13% -> 0% of each run, Pallas kernels for 0% -> 0%
where the time goes in v2:
time: 513 us; the launch traced here: 506 us
  Pallas kernels  460 us (90%)
  local copies, waits for them, and re-layouts  29.1 us (6%)
  other arithmetic  15.3 us (3%)
    pallas_call x5, Pallas kernels, on_core(): pl.pallas_call(kernel, out_shape=[jax.ShapeDtypeStruct(shape, kind) for s...  207 us
    pallas_call x1, Pallas kernels, reduce_grads(): pl.pallas_call(functools.partial(reduce_kernel, chunks, count), out_shape...  163 us
    pallas_call x1, Pallas kernels, gather_weights(): pl.pallas_call(functools.partial(gather_kernel, chunks, count), out_shape...  90.4 us
    unnamed x60, local copies, waits for them, and re-layouts  11.3 us

profile of v2, /device:TPU:0, one launch (start us, length us, event | category | flops | bytes accessed | tf_op | source)
XLA Modules:
  0.0 506.0 jit_solution(3675403469092774294)
XLA Ops:
  0.7 4.8 constant_dynamic-slice_fusion
  5.5 1.6 copy.54
  7.2 0.0 copy-start.23
  7.2 0.0 copy-start.4
  7.2 2.1 pad.18.near
  9.3 0.1 copy.49
  9.4 0.1 reduce
  9.5 0.2 compare_reduce_fusion
  9.7 0.8 fusion
  10.5 0.6 pad_convert_fusion.cell_ok
  11.1 0.2 convert_reduce_fusion
  11.3 0.5 broadcast_subtract_fusion.image
  11.8 0.1 dynamic_slice.17
  11.9 0.1 reshape.201
  12.0 0.1 broadcast_in_dim.2
  12.1 0.1 reshape.202
  12.2 0.1 broadcast_compare_fusion
  12.2 0.8 and_convert_fusion.pair_ok
  13.0 0.1 slice_bitcast_fusion.10
  13.1 1.1 pad_maximum_fusion.2.refs_0_
  14.2 0.1 copy-done.5
  14.3 0.1 slice_bitcast_fusion.7
  14.4 0.0 copy-start.7
  14.4 0.9 pad_maximum_fusion.3.refs_2_
  15.3 0.5 copy-done.3
  15.9 1.7 copy.51
  17.6 0.9 pad_maximum_fusion.4.refs_1_
  18.4 0.6 pad.21.refs_5_
  19.0 90.4 %gather_weights.1 = (bf16[4,768,768]{2,1,0:T(8,128)(2,1)}, bf16[4,384,768]{2,1,0:T(8,128)(2,1)}, bf16[4,384,1024]{2,1,0:T(8,128)(2,1)}, bf16[4,768,768]{2,1,0:T(...) custom-call(bf16[768,768]{1,0:T(8,128)(2,1)} %pad_maximum_fusion.2.refs_0_, ...), custom_call_target="tpu_custom_call" | custom-call | tf_op jit(solution)/shard_map/gather_weights/pallas_call | solution.py:186
  109.5 0.6 reshape.205.first_gain
  110.1 0.6 reshape.207.second_gain
  110.7 0.6 reshape.206.first_shift
  111.2 0.6 reshape.208.second_shift
  111.8 69.1 %forward.1 = (bf16[640,768]{1,0:T(8,128)(2,1)}, bf16[640,768]{1,0:T(8,128)(2,1)}, bf16[640,768]{1,0:T(8,128)(2,1)}, bf16[8,6,160,80]{3,2,1,0:T(8,128)(2,1)}, bf1...) custom-call(s32[16]{0:T(128)} %broadcast_subtract_fusion.image, ...), custom_call_target="tpu_custom_call" | custom-call | tf_op jit(solution)/shard_map/forward/pallas_call | solution.py:698
  181.0 0.6 copy.57
  181.6 0.6 reshape.210.gain
  182.2 0.6 reshape.211.shift
  182.7 43.3 %feed.1 = (bf16[640,768]{1,0:T(8,128)(2,1)}, bf16[4,768,768]{2,1,0:T(8,128)(2,1)}, bf16[4,768,768]{2,1,0:T(8,128)(2,1)}, f32[4,768]{1,0:T(4,128)}, f32[1,768]{1,...) custom-call(f32[640,768]{1,0:T(8,128)} %get-tuple-element.67.second_value, ...), custom_call_target="tpu_custom_call" | custom-call | tf_op jit(solution)/shard_map/feed/pallas_call | solution.py:698
  226.1 58.2 %cross_back.1 = (bf16[4,384,768]{2,1,0:T(8,128)(2,1)}, bf16[4,384,1024]{2,1,0:T(8,128)(2,1)}, bf16[4,10,160,256]{3,2,1,0:T(8,128)(2,1)}, f32[1,768]{1,0:T(1,128)}, f32[1,768]{1,0:T(1,128)}, /*index=5*/f32[640,768]{1,0:T(8,128)}) custom-call(s32[16]{0:T(128)} %broadcast_subtract_fusion.image, bf16[10,160,1024]{2,1,0:T(8,128)(2,1)} %pad.18.near, ...), custom_call_target="tpu_custom_call" | custom-call | tf_op jit(solution)/shard_map/cross_back/pallas_call | solution.py:698
  284.3 32.2 %self_back.1 = (bf16[4,768,768]{2,1,0:T(8,128)(2,1)}, f32[1,768]{1,0:T(1,128)}, f32[1,768]{1,0:T(1,128)}, f32[640,768]{1,0:T(8,128)}) custom-call(bf16[640,768]{1,0:T(8,128)(2,1)} %bitcast.80, bf16[4,768,768]{2,1,0:T(8,128)(2,1)} %get-tuple-element.64.self_weights, bf16[640,768]{1,0:T(8,128)(2,1)} %get-tuple-element.73.queries, ...), custom_call_target="tpu_custom_call" | custom-call | tf_op jit(solution)/shard_map/self_back/pallas_call | solution.py:698
  316.5 0.7 reduce.2
  317.3 0.7 reduce.3
  318.2 0.6 pad.22.refs_6_
  318.8 162.8 %reduce_grads.1 = (bf16[768,768]{1,0:T(8,128)(2,1)}, bf16[384,768]{1,0:T(8,128)(2,1)}, bf16[384,1024]{1,0:T(8,128)(2,1)}, bf16[768,768]{1,0:T(8,128)(2,1)}, bf16...) custom-call(bf16[4,768,768]{2,1,0:T(8,128)(2,1)} %get-tuple-element.91.refs_0_, ...), custom_call_target="tpu_custom_call" | custom-call | tf_op jit(solution)/shard_map/reduce_grads/pallas_call | solution.py:397
  481.6 1.3 convert_element_type.32
  482.9 0.2 slice_bitcast_fusion.1
  483.1 1.2 pad_maximum_fusion.1
  484.4 0.6 copy-done
  484.9 0.2 convert_element_type.30
  485.1 0.1 slice_bitcast_fusion.5
  485.2 1.3 pad_maximum_fusion
  486.6 0.5 iota_multiply_fusion.starts
  487.1 4.2 place.1
  491.3 4.0 copy.52
  495.3 0.2 convert_bitcast_fusion
  495.5 2.0 copy.53
  497.4 2.9 convert_element_type.33
  500.3 0.1 convert_element_type.31
  500.4 0.9 slice_bitcast_fusion.2
  501.3 0.9 slice.117
  502.1 0.9 slice.121
  503.0 0.8 slice_bitcast_fusion.11
  503.7 0.7 dynamic_slice.19
  504.4 1.4 slice_bitcast_fusion.13
  (60 shorter events, 0.3 us)
Async XLA Ops:
  7.2 2.1 copy-start.22
  7.2 4.6 copy-start.23
  7.2 5.8 %copy-start.4 = (bf16[3,768,192]{1,2,0:T(8,128)(2,1)S(1)}, bf16[3,768,192]{1,2,0:T(8,128)(2,1)}, u32[]{:S(2)}) copy-start(bf16[3,768,192]{1,2,0:T(8,128)(2,1)} %param.27) | copy-start | bytes 2654212
  9.3 3.8 copy-start.6
  13.0 1.3 copy-start.5
  14.3 1.6 copy-start.3
  14.4 3.2 copy-start.7
  14.4 3.2 copy-start.8
  15.9 2.6 copy-start.17
  19.0 90.4 %copy-start.11 = (f32[768]{0:T(1024)S(1)}, f32[768]{0:T(1024)}, u32[]{:S(2)}) copy-start(f32[768]{0:T(1024)} %param.29) | copy-start | bytes 9220
  19.0 91.0 %copy-start.12 = (f32[768]{0:T(1024)S(1)}, f32[768]{0:T(1024)}, u32[]{:S(2)}) copy-start(f32[768]{0:T(1024)} %param.34) | copy-start | bytes 9220
  19.0 91.6 %copy-start.13 = (f32[768]{0:T(1024)S(1)}, f32[768]{0:T(1024)}, u32[]{:S(2)}) copy-start(f32[768]{0:T(1024)} %param.30) | copy-start | bytes 9220
  19.0 92.2 %copy-start.14 = (f32[768]{0:T(1024)S(1)}, f32[768]{0:T(1024)}, u32[]{:S(2)}) copy-start(f32[768]{0:T(1024)} %param.35) | copy-start | bytes 9220
  111.8 69.1 %copy-start.9 = (f32[4,8,128]{2,1,0:T(8,128)S(1)}, f32[4,8,128]{2,1,0:T(8,128)}, u32[]{:S(2)}) copy-start(f32[4,8,128]{2,1,0:T(8,128)} %get-tuple-element.71) | copy-start | bytes 49156
  111.8 69.8 %copy-start.15 = (f32[768]{0:T(1024)S(1)}, f32[768]{0:T(1024)}, u32[]{:S(2)}) copy-start(f32[768]{0:T(1024)} %param.39) | copy-start | bytes 9220
  111.8 70.3 %copy-start.16 = (f32[768]{0:T(1024)S(1)}, f32[768]{0:T(1024)}, u32[]{:S(2)}) copy-start(f32[768]{0:T(1024)} %param.40) | copy-start | bytes 9220
  284.3 33.0 %copy-start.10 = (f32[4,768]{1,0:T(4,128)S(1)}, f32[4,768]{1,0:T(4,128)}, u32[]{:S(2)}) copy-start(f32[4,768]{1,0:T(4,128)} %get-tuple-element.97) | copy-start | bytes 36868
  284.3 33.7 %copy-start.21 = (f32[1,768]{1,0:T(1,128)S(1)}, f32[1,768]{1,0:T(1,128)}, u32[]{:S(2)}) copy-start(f32[1,768]{1,0:T(1,128)} %get-tuple-element.100) | copy-start | bytes 9220
  284.3 33.8 %copy-start.20 = (f32[1,768]{1,0:T(1,128)S(1)}, f32[1,768]{1,0:T(1,128)}, u32[]{:S(2)}) copy-start(f32[1,768]{1,0:T(1,128)} %get-tuple-element.101) | copy-start | bytes 9220
  284.3 33.8 %copy-start.19 = (f32[1,768]{1,0:T(1,128)S(1)}, f32[1,768]{1,0:T(1,128)}, u32[]{:S(2)}) copy-start(f32[1,768]{1,0:T(1,128)} %get-tuple-element.102) | copy-start | bytes 9220
  284.3 33.8 %copy-start.18 = (f32[1,768]{1,0:T(1,128)S(1)}, f32[1,768]{1,0:T(1,128)}, u32[]{:S(2)}) copy-start(f32[1,768]{1,0:T(1,128)} %get-tuple-element.103) | copy-start | bytes 9220
  483.1 1.8 copy-start
  491.3 4.0 copy-start.2
  497.4 2.9 copy-start.1

commit v3 on v2

--- a/solution.py
+++ b/solution.py
@@ -61,9 +61,9 @@
 class Gather:
     stages = 4
 
-    def __init__(self, chunks, shards, wholes, sems, window):
+    def __init__(self, chunks, shards, wholes, sems, window, gap):
         self.chunks, self.shards, self.wholes, self.window = chunks, shards, wholes, window
-        self.sems = sems
+        self.sems, self.gap = sems, gap
         self.index, self.plane, self.y, self.x, self.c = place()
         self.core, self.across, self.along, self.planes = partners(self.index, self.plane)
         self.others = [lax.rem(self.plane + step, 4) for step in (1, 2, 3)]
@@ -71,17 +71,18 @@
 
     def sizes(self, k):
         which, base, rows = self.chunks[k]
-        return which, base, rows // 8, self.shards[which].shape[1] // 2
+        return which, base, rows // 8, self.wholes[which].shape[2] // 2
 
     def level(self, k):
         which, base, r, w = self.sizes(k)
         _, _, send, recv = self.sems[:4]
+        self.own(which)
         items = []
         for h, first in enumerate((self.x * 2 + self.y, self.y * 2 + self.x)):
             here = (pl.ds(pl.multiple_of(base + (self.c * 4 + first) * r, 16), r), pl.ds(h * w, w))
             for j, peer in enumerate(self.planes):
-                target = self.wholes[which].at[(self.plane,) + here]
-                items.append((self.shards[which].at[here], target, send.at[k, h, j], recv.at[k, h, j], peer))
+                piece = self.wholes[which].at[(self.plane,) + here]
+                items.append((piece, piece, send.at[k, h, j], recv.at[k, h, j], peer))
         self.sends.start("level", k, items)
 
     def near(self, k):
@@ -121,28 +122,35 @@
             items.append((piece, piece, send.at[k, j], recv.at[k, j], self.core))
         self.sends.start("core", k, items)
 
+    def own(self, which):
+        for copy in self.local.pop(which, ()):
+            copy.wait()
+
     def begin(self):
+        self.local = {}
+        for which, pieces in enumerate(self.shards):
+            row, self.local[which] = 0, []
+            for i, piece in enumerate(pieces):
+                target = self.wholes[which].at[self.plane, pl.ds(row, piece.shape[0]), :]
+                copy = pltpu.make_async_copy(piece, target, self.sems[0].at[which, i])
+                copy.start()
+                self.local[which].append(copy)
+                row += piece.shape[0]
         greet([self.core, self.across, self.along] + self.planes)
         for k in range(self.window):
             self.level(k)
-        local_sem = self.sems[0]
-        self.local = []
-        for which, shard in enumerate(self.shards):
-            copy = pltpu.make_async_copy(shard, self.wholes[which].at[self.plane], local_sem.at[which])
-            copy.start()
-            self.local.append(copy)
 
     def step(self, t):
-        if 0 <= t - 4 < len(self.chunks):
-            self.cross(t - 4)
-        if 0 <= t - 2 < len(self.chunks):
-            self.far(t - 2)
+        if 0 <= t - 2 * self.gap < len(self.chunks):
+            self.cross(t - 2 * self.gap)
+        if 0 <= t - self.gap < len(self.chunks):
+            self.far(t - self.gap)
         if 0 <= t < len(self.chunks):
             self.near(t)
 
     @property
     def steps(self):
-        return len(self.chunks) + 4
+        return len(self.chunks) + 2 * self.gap
 
     def ready(self, k):
         self.sends.arrived("core", k)
@@ -150,51 +158,105 @@
     @staticmethod
     def scratch(count, total):
         dma = pltpu.SemaphoreType.DMA
-        return [dma((count,)), dma((count,))] + [dma((total, 2, 3))] * 6 + [dma((total, 3))] * 2
-
-
-def gather_kernel(chunks, count, *refs):
-    shards, bias, outs, biases = refs[:count], refs[count], refs[count + 1 : 2 * count + 1], refs[2 * count + 1]
-    rest = refs[2 * count + 2 :]
-    wholes, bias_send, bias_recv, sems = rest[:count], rest[count], rest[count + 1], rest[count + 2 :]
-    gather = Gather(chunks, shards, wholes, sems, 3)
+        return [dma((count, 2)), dma((count,))] + [dma((total, 2, 3))] * 6 + [dma((total, 3))] * 2
+
+
+class Ticks:
+    def __init__(self, gather, outs, sem):
+        self.gather, self.outs, self.sem = gather, outs, sem
+        self.now, self.done, self.final = 0, 0, []
+
+    def __call__(self):
+        gather, total = self.gather, len(self.gather.chunks)
+        if self.now < gather.steps:
+            gather.step(self.now)
+        k = self.now - 3 * gather.gap
+        if 0 <= k < total:
+            gather.ready(k)
+            self.done = k + 1
+            which = gather.chunks[k][0]
+            if k + 1 == total or gather.chunks[k + 1][0] != which:
+                copy = pltpu.make_async_copy(gather.wholes[which], self.outs[which], self.sem.at[which])
+                copy.start()
+                self.final.append(copy)
+        self.now += 1
+
+    def wait(self, which):
+        last = max(k for k, chunk in enumerate(self.gather.chunks) if chunk[0] == which)
+        while self.done <= last:
+            self()
+
+    def close(self):
+        while self.done < len(self.gather.chunks):
+            self()
+        self.gather.sends.close()
+        for copy in self.final:
+            copy.wait()
+
+
+def forward_kernel(chunks, pieces, window, count, *refs):
+    image, tokens, pair_ok, cell_ok, norms, patches = refs[:6]
+    refs, shards, arrays = refs[6:], [], len(pieces)
+    for amount in pieces:
+        shards.append(refs[:amount])
+        refs = refs[amount:]
+    outs, biases, far, refs = refs[:arrays], refs[arrays], refs[arrays + 1 : arrays + 1 + count], refs[arrays + 1 + count :]
+    wholes, refs = refs[:arrays], refs[arrays:]
+    saved = [Slot(far[i], refs[2 * i], refs[2 * i + 1]) for i in range(count)]
+    (wide, near, bias_send, bias_recv, near_sem), sems = refs[2 * count : 2 * count + 5], refs[2 * count + 5 :]
+    gather = Gather(chunks, shards, wholes, sems, 3, 1)
     gather.begin()
     gather.sends.start(
-        "bias", 0, [(bias, biases.at[gather.plane], bias_send.at[j], bias_recv.at[j], peer) for j, peer in enumerate(gather.planes)]
+        "bias", 0, [(norms, biases.at[gather.plane], bias_send.at[j], bias_recv.at[j], peer) for j, peer in enumerate(gather.planes)]
     )
-    biases[gather.plane] = bias[...]
-    final = []
-    for t in range(gather.steps + 2):
-        if 0 <= t - 6 < len(chunks):
-            gather.ready(t - 6)
-            which = chunks[t - 6][0]
-            if t - 5 == len(chunks) or chunks[t - 5][0] != which:
-                gather.local[which].wait()
-                copy = pltpu.make_async_copy(wholes[which], outs[which], sems[1].at[which])
-                copy.start()
-                final.append(copy)
-        gather.step(t)
+    start = jnp.minimum(gather.plane * cell_ok.shape[0] // ROWS_MAX, patches.shape[0] - window)
+    copy = pltpu.make_async_copy(patches.at[pl.ds(start, window)], near, near_sem)
+    copy.start()
+    biases[gather.plane] = norms[...]
+    copy.wait()
+    ticks = Ticks(gather, outs, sems[1])
+    forward_steps(ticks, image, tokens, near, pair_ok, cell_ok, wholes[:3], norms, saved, wide)
     gather.sends.arrived("bias", 0)
-    gather.sends.close()
-    for copy in final:
-        copy.wait()
-
-
-def gather_weights(shards, bias, chunks):
-    count, dma = len(shards), pltpu.SemaphoreType.DMA
+    ticks.close()
+    for slot in saved:
+        slot.finish()
+
+
+def gather_forward(image, inputs, patches, shards, window, outputs, chunks):
+    dma, bf16, arrays, count = pltpu.SemaphoreType.DMA, jnp.bfloat16, len(shards), len(outputs)
     any_space, vmem = pl.BlockSpec(memory_space=pl.ANY), pl.BlockSpec(memory_space=pltpu.VMEM)
-    *wholes, biases = pl.pallas_call(
-        functools.partial(gather_kernel, chunks, count),
-        out_shape=[jax.ShapeDtypeStruct((4,) + s.shape, s.dtype) for s in shards + [bias]],
-        in_specs=[any_space] * count + [vmem],
-        out_specs=[any_space] * count + [vmem],
-        scratch_shapes=[pltpu.VMEM((4,) + s.shape, s.dtype) for s in shards]
-        + [dma((3,)), dma((3,))]
-        + Gather.scratch(count, len(chunks)),
-        compiler_params=pltpu.CompilerParams(collective_id=0, has_side_effects=True, vmem_limit_bytes=62 << 20),
-        name="gather_weights",
-    )(*shards, bias)
-    return wholes, biases
+    tokens, norms = inputs[0], inputs[-1]
+    shapes = [(4, sum(piece.shape[0] for piece in pieces), pieces[0].shape[1]) for pieces in shards]
+    flat = [piece for pieces in shards for piece in pieces]
+    results = pl.pallas_call(
+        functools.partial(forward_kernel, chunks, [len(pieces) for pieces in shards], window, count),
+        out_shape=[jax.ShapeDtypeStruct(shape, bf16) for shape in shapes]
+        + [jax.ShapeDtypeStruct((4,) + norms.shape, norms.dtype)]
+        + [jax.ShapeDtypeStruct(shape, kind) for shape, kind in outputs],
+        in_specs=[pl.BlockSpec(memory_space=pltpu.SMEM)] + [vmem] * len(inputs) + [any_space] * (len(flat) + 1),
+        out_specs=[any_space] * arrays + [vmem] + [any_space] * count,
+        scratch_shapes=[pltpu.VMEM(shape, bf16) for shape in shapes]
+        + [entry for shape, kind in outputs for entry in slot_scratch(shape, kind)]
+        + [pltpu.VMEM(tokens.shape, jnp.float32), pltpu.VMEM((window,) + patches.shape[1:], bf16)]
+        + [dma((3,)), dma((3,)), dma(())]
+        + Gather.scratch(arrays, len(chunks)),
+        compiler_params=pltpu.CompilerParams(collective_id=0, has_side_effects=True, vmem_limit_bytes=63 << 20),
+        name="gather_forward",
+    )(image, *inputs, patches, *flat)
+    return results[:arrays], results[arrays], results[arrays + 1 :]
+
+
+class Alone:
+    def __call__(self):
+        pass
+
+    def wait(self, which):
+        pass
+
+
+def lone_forward_kernel(image, inputs, outputs, scratch):
+    tokens, pair_ok, cell_ok, norms, near, *weights = (slot.ready() for slot in inputs)
+    forward_steps(Alone(), image, tokens, near, pair_ok, cell_ok, weights, norms, outputs, scratch[0])
 
 
 class Reduce:
@@ -409,6 +471,70 @@
     return sums, windows, vector_sum[4]
 
 
+class Slot:
+    def __init__(self, far, near, sem, parts=0):
+        self.far, self.near, self.sem, self.parts, self.waited = far, near, sem, parts, False
+
+    def copy(self, out, m=None):
+        far, near = (self.far, self.near) if m is None else (self.far.at[m], self.near.at[m])
+        sem = self.sem.at[0 if m is None else m]
+        return pltpu.make_async_copy(near, far, sem) if out else pltpu.make_async_copy(far, near, sem)
+
+    def fetch(self):
+        for m in range(self.parts) if self.parts else (None,):
+            self.copy(False, m).start()
+
+    def ready(self):
+        if not self.waited:
+            self.waited = True
+            for m in range(self.parts) if self.parts else (None,):
+                self.copy(False, m).wait()
+        return self.near
+
+    def flush(self, m=None):
+        self.copy(True, m).start()
+
+    def finish(self):
+        for m in range(self.parts) if self.parts else (None,):
+            self.copy(True, m).wait()
+
+
+def slot_scratch(shape, kind, parts=0):
+    return [pltpu.VMEM(shape, kind), pltpu.SemaphoreType.DMA((max(parts, 1),))]
+
+
+def on_slots(kernel, name, image, inputs, outputs, scratch, parts_in=(), parts_out=()):
+    count, total = len(inputs), len(inputs) + len(outputs)
+
+    def body(image_ref, *refs):
+        far, refs = refs[:total], refs[total:]
+        slots = []
+        for i in range(total):
+            parts = far[i].shape[0] if (i in parts_in if i < count else i - count in parts_out) else 0
+            slots.append(Slot(far[i], refs[2 * i], refs[2 * i + 1], parts))
+        for slot in slots[:count]:
+            slot.fetch()
+        kernel(image_ref, slots[:count], slots[count:], refs[2 * total :])
+        for slot in slots[count:]:
+            slot.finish()
+
+    spaces = []
+    for i, array in enumerate(inputs):
+        spaces += slot_scratch(array.shape, array.dtype, array.shape[0] if i in parts_in else 0)
+    for i, (shape, kind) in enumerate(outputs):
+        spaces += slot_scratch(shape, kind, shape[0] if i in parts_out else 0)
+    any_space = pl.BlockSpec(memory_space=pl.ANY)
+    return pl.pallas_call(
+        body,
+        out_shape=[jax.ShapeDtypeStruct(shape, kind) for shape, kind in outputs],
+        in_specs=[pl.BlockSpec(memory_space=pltpu.SMEM)] + [any_space] * count,
+        out_specs=[any_space] * len(outputs),
+        scratch_shapes=spaces + [pltpu.VMEM(shape, kind) for shape, kind in scratch],
+        compiler_params=pltpu.CompilerParams(vmem_limit_bytes=63 << 20),
+        name=name,
+    )(image, *inputs)
+
+
 def nn(left, right):
     return lax.dot_general(left, right, (((1,), (0,)), ((), ())), preferred_element_type=jnp.float32)
 
@@ -489,198 +615,278 @@
     return (raised * (1.0 / jnp.sum(raised, axis=-1, keepdims=True))).astype(jnp.bfloat16)
 
 
-def attend_self(queries, keys, values, pair_ok, probs, context):
+def columns(width):
+    return [slice(start, start + 128) for start in range(0, width, 128)]
+
+
+def stack(value, first, second):
+    return jnp.concatenate([value * first, value * second], axis=0)
+
+
+def merge(low, value):
+    half = value.shape[0] // 2
+    return jnp.where(low, value[:half], value[half:])
+
+
+def attend_self(queries, keys, values, pair_ok, probs, context, begin, end):
     low, first, second = lanes()
-    first_low, second_low = first.astype(jnp.bfloat16), second.astype(jnp.bfloat16)
-
-    @pl.loop(0, pair_ok.shape[0])
+    first, second = first.astype(jnp.bfloat16), second.astype(jnp.bfloat16)
+    cols = columns(queries.shape[1])
+
+    @pl.loop(begin, end)
     def _(pair):
         rows = pl.ds(pl.multiple_of(pair * 80, 80), 80)
         allowed = pair_ok[pair] > 0
         allowed = jnp.concatenate([allowed, allowed], axis=0)
-        for tile in range(6):
-            cols = slice(tile * 128, (tile + 1) * 128)
-            query = queries[rows, cols]
-            both = jnp.concatenate([query * first_low, query * second_low], axis=0)
-            scores = jnp.where(allowed, nt(both, keys[rows, cols]) * HEAD_DIM ** (-0.5), -1000000000.0)
-            weights = softmax(scores)
-            probs[pair, tile] = weights
-            mixed = nn(weights, values[rows, cols])
-            context[rows, cols] = jnp.where(low, mixed[:80], mixed[80:]).astype(jnp.bfloat16)
-
-
-def attend_cross(image, wide, keys, values, cell_ok, probs):
+        stacked = [stack(queries[rows, c], first, second) for c in cols]
+        scores = [nt(both, keys[rows, c]) * HEAD_DIM ** (-0.5) for both, c in zip(stacked, cols)]
+        weights = [softmax(jnp.where(allowed, score, -1000000000.0)) for score in scores]
+        mixed = [merge(low, nn(weight, values[rows, c])) for weight, c in zip(weights, cols)]
+        for tile, c in enumerate(cols):
+            probs[pair, tile] = weights[tile]
+            context[rows, c] = mixed[tile].astype(jnp.bfloat16)
+
+
+def attend_cross(image, wide, keys, values, cell_ok, probs, begin, end):
     low, first, second = lanes()
-
-    @pl.loop(0, cell_ok.shape[0])
+    cols = columns(wide.shape[1])
+
+    @pl.loop(begin, end)
     def _(row):
         rows = pl.ds(pl.multiple_of(row * 40, 40), 40)
         which = image[row]
         allowed = jnp.broadcast_to(cell_ok[pl.ds(row, 1), :], (80, cell_ok.shape[1])) > 0
-        for tile in range(6):
-            cols = slice(tile * 128, (tile + 1) * 128)
-            query = wide[rows, cols]
-            both = jnp.concatenate([query * first, query * second], axis=0).astype(jnp.bfloat16)
-            scores = jnp.where(allowed, nt(both, keys[which, :, cols]) * HEAD_DIM ** (-0.5), -1000000000.0)
-            weights = softmax(scores)
-            probs[row, tile] = weights
-            mixed = nn(weights, values[which, :, cols])
-            wide[rows, cols] = jnp.where(low, mixed[:40], mixed[40:])
-
-
-def forward_kernel(
-    image, tokens, near, pair_ok, cell_ok, self_weights, cross_weights, keyval, first_gain, first_shift, second_gain,
-    second_shift,
-    queries, keys, values, self_probs, self_context, first_unit, first_inverse, first_low, cross_queries, image_keys,
-    image_values, cross_probs, cross_context, second_unit, second_inverse, second_value, second_low,
-    total, first_value, wide,
-):
+        stacked = [stack(wide[rows, c], first, second).astype(jnp.bfloat16) for c in cols]
+        scores = [nt(both, keys[which, :, c]) * HEAD_DIM ** (-0.5) for both, c in zip(stacked, cols)]
+        weights = [softmax(jnp.where(allowed, score, -1000000000.0)) for score in scores]
+        mixed = [merge(low, nn(weight, values[which, :, c])) for weight, c in zip(weights, cols)]
+        for tile, c in enumerate(cols):
+            probs[row, tile] = weights[tile]
+            wide[rows, c] = mixed[tile]
+
+
+def forward_steps(ticks, image, tokens, near, pair_ok, cell_ok, weights, norms, saved, wide):
     bf16 = jnp.bfloat16
+    self_weights, cross_weights, keyval = weights
+    (
+        queries, keys, values, self_probs, self_context, first_unit, first_inverse, first_low, cross_queries, image_keys,
+        image_values, cross_probs, cross_context, second_unit, second_inverse, second_value, second_low,
+    ) = (slot.near for slot in saved)
+
+    def flush(*places):
+        for place in places:
+            saved[place].flush()
+
+    gains = [norms.at[pl.ds(i, 1), :] for i in range(4)]
+    ticks.wait(0)
     for target, which in ((queries, 0), (keys, 1), (values, 2)):
         target[...] = nt(tokens[...], part(self_weights, which)).astype(bf16)
-    attend_self(queries, keys, values, pair_ok, self_probs, self_context)
-    total[...] = nn(self_context[...], part(self_weights, 3)) + tokens[...].astype(jnp.float32)
-    norm_forward(total, first_unit, first_inverse, first_value, first_low, first_gain, first_shift)
+    flush(0, 1, 2)
+    ticks()
+    pairs = pair_ok.shape[0]
+    attend_self(queries, keys, values, pair_ok, self_probs, self_context, 0, pairs)
+    flush(3, 4)
+    ticks()
+    second_value[...] = nn(self_context[...], part(self_weights, 3)) + tokens[...].astype(jnp.float32)
+    norm_forward(second_value, first_unit, first_inverse, None, first_low, gains[0], gains[1])
+    flush(5, 6, 7)
+    ticks.wait(1)
     cross_queries[...] = nt(first_low[...], part(cross_weights, 0)).astype(bf16)
+    flush(8)
     wide[...] = cross_queries[...].astype(jnp.float32)
     images, cells, depth = near.shape
     half = images // 2
+    ticks.wait(2)
     for target, which in ((image_keys, 0), (image_values, 1)):
         weight = part(keyval, which)
         for step in range(2):
             block = near[step * half : (step + 1) * half].reshape(half * cells, depth)
             target[step * half : (step + 1) * half] = nt(block, weight).astype(bf16).reshape(half, cells, -1)
-    attend_cross(image, wide, image_keys, image_values, cell_ok, cross_probs)
+        flush(9 + which)
+    ticks()
+    rows = cell_ok.shape[0]
+    for part_of in range(2):
+        begin, end = part_of * rows // 2, (part_of + 1) * rows // 2
+        attend_cross(image, wide, image_keys, image_values, cell_ok, cross_probs, begin, end)
+        ticks()
+    flush(11)
     cross_context[...] = wide[...].astype(bf16)
-    total[...] = nn(cross_context[...], part(cross_weights, 1)) + first_value[...]
-    norm_forward(total, second_unit, second_inverse, second_value, second_low, second_gain, second_shift)
-
-
-def feed_kernel(
-    second_value, second_low, expand, shrink, bias, gain, shift, cotangent,
-    joined, expand_grad, shrink_grad, bias_grad, gain_grad, shift_grad, second_up,
-    active, slope, wide, unit, inverse, feed_low,
-):
+    flush(12)
+    second_value[...] = nn(cross_context[...], part(cross_weights, 1)) + (first_unit[...] * gains[0][...] + gains[1][...])
+    norm_forward(second_value, second_unit, second_inverse, second_value, second_low, gains[2], gains[3])
+    flush(13, 14, 15, 16)
+
+
+def feed_kernel(image, inputs, outputs, scratch):
+    second_value, second_low, norms, biases, expand, shrink, cotangent = inputs
+    joined, expand_grad, shrink_grad, vectors, second_up = outputs
+    active, slope, wide, unit, inverse, feed_low = scratch
     bf16 = jnp.bfloat16
-    second_up[...] = second_value[...]
-
-    @pl.loop(0, 4)
+    total = second_up.near
+    total[...] = second_value.ready()[...]
+    second_low, norms, biases = second_low.ready(), norms.ready(), biases.ready()
+    gain, shift = norms.at[pl.ds(4, 1), :], norms.at[pl.ds(5, 1), :]
+    hidden = expand.near.shape[0]
+
+    @pl.loop(0, hidden)
     def _(m):
-        wide[...] = nt(second_low[...], expand[m])
-
-        @tiles(wide.shape[0], 40)
+        expand.copy(False, m).wait()
+        wide[...] = nn(second_low[...], expand.near[m])
+
+        @tiles(wide.shape[0], 80)
         def _(rows):
-            inner = wide[rows, :] + bias[pl.ds(m, 1), :]
+            inner = wide[rows, :] + biases[m, pl.ds(6, 1), :]
             share = 0.5 * (1.0 + lax.erf(inner * 0.5**0.5))
-            wide[rows, :] = inner * share
-            unit[rows, :] = share + inner * (jnp.exp(-0.5 * inner * inner) * 0.3989422804014327)
-
-        active[m] = wide[...].astype(bf16)
-        slope[m] = unit[...].astype(bf16)
-        second_up[...] += nn(active[m], shrink[m])
-
-    norm_forward(second_up, unit, inverse, None, joined, gain, shift)
-    norm_reverse(cotangent, unit, inverse, gain, gain_grad, shift_grad, second_up, feed_low)
-
-    @pl.loop(0, 4)
+            active[m, rows, :] = (inner * share).astype(bf16)
+            slope[m, rows, :] = (share + inner * (jnp.exp(-0.5 * inner * inner) * 0.3989422804014327)).astype(bf16)
+
+        shrink.copy(False, m).wait()
+        total[...] += nn(active[m], shrink.near[m])
+
+    norm_forward(total, unit, inverse, None, joined.near, gain, shift)
+    joined.flush()
+    sums = vectors.near
+    sums[...] = jnp.zeros_like(sums)
+    norm_reverse(
+        cotangent.ready(), unit, inverse, gain, sums.at[pl.ds(8, 1), :], sums.at[pl.ds(9, 1), :], total, feed_low
+    )
+
+    @pl.loop(0, hidden)
     def _(m):
-        shrink_grad[m] = tn(active[m], feed_low[...]).astype(bf16)
-        wide[...] = nt(feed_low[...], shrink[m])
-        bias_grad[pl.ds(m, 1), :] = jnp.zeros((1, 768), jnp.float32)
+        shrink_grad.near[m] = tn(active[m], feed_low[...]).astype(bf16)
+        shrink_grad.flush(m)
+        wide[...] = nt(feed_low[...], shrink.near[m])
 
         @tiles(wide.shape[0], 80)
         def _(rows):
             low = (wide[rows, :] * slope[m, rows, :].astype(jnp.float32)).astype(bf16)
             active[m, rows, :] = low
-            bias_grad[pl.ds(m, 1), :] += jnp.sum(low.astype(jnp.float32), axis=0, keepdims=True)
-
-        expand_grad[m] = tn(active[m], second_low[...]).astype(bf16)
-        second_up[...] += nn(active[m], expand[m])
-
-
-def cross_back_kernel(
-    image, near, cross_weights, keyval, cross_queries, image_keys, image_values, cross_probs, cross_context, second_up,
-    second_unit, second_inverse, second_gain, first_low,
-    weights_grad, keyval_grad, patch_part, gain_grad, shift_grad, first_up,
-    grad_low, wide, turn, key_sum, value_sum, query_low,
-):
+            sums[pl.ds(m, 1), :] += jnp.sum(low.astype(jnp.float32), axis=0, keepdims=True)
+
+        expand_grad.near[m] = tn(second_low[...], active[m]).astype(bf16)
+        expand_grad.flush(m)
+        total[...] += nt(active[m], expand.near[m])
+
+    vectors.flush()
+    second_up.flush()
+
+
+def score_back(weights, upstream):
+    probs = weights.astype(jnp.float32)
+    return (probs * (upstream - jnp.sum(probs * upstream, axis=-1, keepdims=True))).astype(jnp.bfloat16)
+
+
+def cross_back_kernel(image, inputs, outputs, scratch):
+    (
+        second_up, second_unit, second_inverse, norms, cross_weights, cross_context, cross_queries, image_values,
+        image_keys, cross_probs, first_low, keyval, near,
+    ) = inputs
+    weights_grad, keyval_grad, patch, vectors, first_up = outputs
+    grad_low, wide, turn, key_sum, value_sum, query_low = scratch
     bf16 = jnp.bfloat16
     low, first, second = lanes()
-    norm_reverse(second_up, second_unit, second_inverse, second_gain, gain_grad, shift_grad, first_up, grad_low)
-    store_part(weights_grad, 1, tn(cross_context[...], grad_low[...]))
+    sums = vectors.near
+    sums[...] = jnp.zeros_like(sums)
+    norm_reverse(
+        second_up.ready(), second_unit.ready(), second_inverse.ready(), norms.ready().at[pl.ds(2, 1), :],
+        sums.at[pl.ds(6, 1), :], sums.at[pl.ds(7, 1), :], first_up.near, grad_low,
+    )
+    vectors.flush()
+    cross_weights = cross_weights.ready()
     wide[...] = nt(grad_low[...], part(cross_weights, 1)).astype(bf16).astype(jnp.float32)
-    turn[...] = cross_queries[...].astype(jnp.float32)
+    store_part(weights_grad.near, 1, tn(cross_context.ready()[...], grad_low[...]))
+    turn[...] = cross_queries.ready()[...].astype(jnp.float32)
     key_sum[...] = jnp.zeros_like(key_sum)
     value_sum[...] = jnp.zeros_like(value_sum)
+    cols = columns(wide.shape[1])
+    image_values, image_keys, cross_probs = image_values.ready(), image_keys.ready(), cross_probs.ready()
 
     @pl.loop(0, cross_probs.shape[0])
     def _(row):
         rows = pl.ds(pl.multiple_of(row * 40, 40), 40)
         which = image[row]
-        for tile in range(6):
-            cols = slice(tile * 128, (tile + 1) * 128)
-            query, grad = turn[rows, cols], wide[rows, cols]
-            queries = jnp.concatenate([query * first, query * second], axis=0).astype(bf16)
-            grads = jnp.concatenate([grad * first, grad * second], axis=0).astype(bf16)
-            weights = cross_probs[row, tile]
-            probs = weights.astype(jnp.float32)
-            upstream = nt(grads, image_values[which, :, cols])
-            back = (probs * (upstream - jnp.sum(probs * upstream, axis=-1, keepdims=True))).astype(bf16)
-            mixed = nn(back, image_keys[which, :, cols])
-            turn[rows, cols] = jnp.where(low, mixed[:40], mixed[40:]) * HEAD_DIM ** (-0.5)
-            key_sum[which, :, cols] += tn(back, queries) * HEAD_DIM ** (-0.5)
-            value_sum[which, :, cols] += tn(weights, grads)
-
-    query_low[...] = turn[...].astype(bf16)
-    store_part(weights_grad, 0, tn(query_low[...], first_low[...]))
-    first_up[...] += nn(query_low[...], part(cross_weights, 0))
+        queries = [stack(turn[rows, c], first, second).astype(bf16) for c in cols]
+        grads = [stack(wide[rows, c], first, second).astype(bf16) for c in cols]
+        weights = [cross_probs[row, tile] for tile in range(len(cols))]
+        upstream = [nt(grad, image_values[which, :, c]) for grad, c in zip(grads, cols)]
+        back = [score_back(weight, up) for weight, up in zip(weights, upstream)]
+        mixed = [merge(low, nn(grad, image_keys[which, :, c])) * HEAD_DIM ** (-0.5) for grad, c in zip(back, cols)]
+        key_parts = [tn(grad, both) * HEAD_DIM ** (-0.5) for grad, both in zip(back, queries)]
+        value_parts = [tn(weight, grad) for weight, grad in zip(weights, grads)]
+        for tile, c in enumerate(cols):
+            turn[rows, c] = mixed[tile]
+        for tile, c in enumerate(cols):
+            key_sum[which, :, c] += key_parts[tile]
+        for tile, c in enumerate(cols):
+            value_sum[which, :, c] += value_parts[tile]
+
+    keyval, near = keyval.ready(), near.ready()
     images, cells, depth = near.shape
     amount = images * cells
-    for source, which in ((key_sum, 0), (value_sum, 1)):
-        flat = source[...].astype(bf16).reshape(amount, -1)
-        store_part(keyval_grad, which, tn(flat, near[...].reshape(amount, depth)))
     for step in range(2):
         here = slice(step * (images // 2), (step + 1) * (images // 2))
         block = nn(key_sum[here].astype(bf16).reshape(amount // 2, -1), part(keyval, 0))
         block += nn(value_sum[here].astype(bf16).reshape(amount // 2, -1), part(keyval, 1))
         block = block.astype(bf16)
-        for m in range(4):
-            patch_part[m, here] = block[:, m * 256 : (m + 1) * 256].reshape(images // 2, cells, 256)
-
-
-def self_back_kernel(
-    tokens, self_weights, queries, keys, values, self_probs, self_context, first_up, first_unit, first_inverse,
-    first_gain,
-    weights_grad, gain_grad, shift_grad, text_grad,
-    grad_low, context_low, query_low, key_low, value_low,
-):
+        quarter = patch.near.shape[3]
+        for m in range(patch.near.shape[0]):
+            patch.near[m, here] = block[:, m * quarter : (m + 1) * quarter].reshape(images // 2, cells, quarter)
+    patch.flush()
+    for source, which in ((key_sum, 0), (value_sum, 1)):
+        flat = source[...].astype(bf16).reshape(amount, -1)
+        store_part(keyval_grad.near, which, tn(flat, near[...].reshape(amount, depth)))
+    keyval_grad.flush()
+    query_low[...] = turn[...].astype(bf16)
+    first_up.near[...] += nn(query_low[...], part(cross_weights, 0))
+    first_up.flush()
+    store_part(weights_grad.near, 0, tn(query_low[...], first_low.ready()[...]))
+    weights_grad.flush()
+
+
+def self_back_kernel(image, inputs, outputs, scratch):
+    (
+        first_up, first_unit, first_inverse, norms, self_weights, self_context, queries, keys, values, self_probs, tokens,
+    ) = inputs
+    weights_grad, vectors, text_grad = outputs
+    grad_low, context_low, query_low, key_low, value_low = scratch
     bf16 = jnp.bfloat16
     low, first, second = lanes()
     first_mask, second_mask = first.astype(bf16), second.astype(bf16)
-    norm_reverse(first_up, first_unit, first_inverse, first_gain, gain_grad, shift_grad, text_grad, grad_low)
-    store_part(weights_grad, 3, tn(self_context[...], grad_low[...]))
+    sums = vectors.near
+    sums[...] = jnp.zeros_like(sums)
+    norm_reverse(
+        first_up.ready(), first_unit.ready(), first_inverse.ready(), norms.ready().at[pl.ds(0, 1), :],
+        sums.at[pl.ds(4, 1), :], sums.at[pl.ds(5, 1), :], text_grad.near, grad_low,
+    )
+    vectors.flush()
+    self_weights = self_weights.ready()
     context_low[...] = nt(grad_low[...], part(self_weights, 3)).astype(bf16)
+    store_part(weights_grad.near, 3, tn(self_context.ready()[...], grad_low[...]))
+    cols = columns(context_low.shape[1])
+    queries, keys, values, self_probs = queries.ready(), keys.ready(), values.ready(), self_probs.ready()
 
     @pl.loop(0, self_probs.shape[0])
     def _(pair):
         rows = pl.ds(pl.multiple_of(pair * 80, 80), 80)
-        for tile in range(6):
-            cols = slice(tile * 128, (tile + 1) * 128)
-            query, grad = queries[rows, cols], context_low[rows, cols]
-            both = jnp.concatenate([query * first_mask, query * second_mask], axis=0)
-            grads = jnp.concatenate([grad * first_mask, grad * second_mask], axis=0)
-            weights = self_probs[pair, tile]
-            probs = weights.astype(jnp.float32)
-            upstream = nt(grads, values[rows, cols])
-            back = (probs * (upstream - jnp.sum(probs * upstream, axis=-1, keepdims=True))).astype(bf16)
-            mixed = nn(back, keys[rows, cols])
-            query_low[rows, cols] = (jnp.where(low, mixed[:80], mixed[80:]) * HEAD_DIM ** (-0.5)).astype(bf16)
-            key_low[rows, cols] = (tn(back, both) * HEAD_DIM ** (-0.5)).astype(bf16)
-            value_low[rows, cols] = tn(weights, grads).astype(bf16)
-
+        stacked = [stack(queries[rows, c], first_mask, second_mask) for c in cols]
+        grads = [stack(context_low[rows, c], first_mask, second_mask) for c in cols]
+        weights = [self_probs[pair, tile] for tile in range(len(cols))]
+        upstream = [nt(grad, values[rows, c]) for grad, c in zip(grads, cols)]
+        back = [score_back(weight, up) for weight, up in zip(weights, upstream)]
+        query_parts = [merge(low, nn(grad, keys[rows, c])) * HEAD_DIM ** (-0.5) for grad, c in zip(back, cols)]
+        key_parts = [tn(grad, both) * HEAD_DIM ** (-0.5) for grad, both in zip(back, stacked)]
+        value_parts = [tn(weight, grad) for weight, grad in zip(weights, grads)]
+        for tile, c in enumerate(cols):
+            query_low[rows, c] = query_parts[tile].astype(bf16)
+            key_low[rows, c] = key_parts[tile].astype(bf16)
+            value_low[rows, c] = value_parts[tile].astype(bf16)
+
+    tokens = tokens.ready()
     for source, which in ((query_low, 0), (key_low, 1), (value_low, 2)):
-        store_part(weights_grad, which, tn(source[...], tokens[...]))
-        text_grad[...] += nn(source[...], part(self_weights, which))
+        store_part(weights_grad.near, which, tn(source[...], tokens[...]))
+        text_grad.near[...] += nn(source[...], part(self_weights, which))
+    weights_grad.flush()
+    text_grad.flush()
 
 
 def place_kernel(starts, windows, result):
@@ -715,10 +921,15 @@
     return [min(start, group_images - window) for start in first], window
 
 
-def gather_shards(shards, bias, chunks, own):
+def forward(image, inputs, patches, shards, start, window, outputs, chunks, own):
     if own:
-        return gather_weights(shards, bias, chunks)
-    return [lax.all_gather(shard, "mp", axis=0) for shard in shards], lax.all_gather(bias, "mp", axis=0)
+        return gather_forward(image, inputs, patches, shards, window, outputs, chunks)
+    weights = [lax.all_gather(jnp.concatenate(pieces, axis=0), "mp", axis=0) for pieces in shards]
+    biases = lax.all_gather(inputs[-1], "mp", axis=0)
+    near = lax.dynamic_slice_in_dim(patches, start, window, 0)
+    scratch = [(inputs[0].shape, jnp.float32)]
+    saved = on_slots(lone_forward_kernel, "forward", image, inputs + [near] + weights[:3], outputs, scratch)
+    return weights, biases, saved
 
 
 def reduce_shards(grads, patch, vectors, chunks, own):
@@ -746,19 +957,17 @@
     start = jnp.asarray(starts, jnp.int32)[plane]
     amount, pairs, tiles_of = rows * slots, rows // 2, width // 128
 
-    inner, hidden = self_output.shape[0], expand_bias.shape[0]
+    inner = self_output.shape[0]
     shards = [
-        jnp.concatenate([self_project[0].T, self_project[1].T, self_project[2].T, self_output], axis=0),
-        jnp.concatenate([cross_query.T, cross_output], axis=0),
-        jnp.concatenate([cross_keyval[0].T, cross_keyval[1].T], axis=0),
-        expand_weight.T,
-        shrink_weight,
+        [self_project.transpose(0, 2, 1).reshape(3 * inner, width), self_output],
+        [cross_query.T, cross_output],
+        [cross_keyval.transpose(0, 2, 1).reshape(2 * inner, depth)],
+        [expand_weight],
+        [shrink_weight],
     ]
     chunks = [(0, 0, 384), (0, 384, 384), (1, 0, 384), (2, 0, 384), (3, 0, 384), (3, 384, 384), (4, 0, 384), (4, 384, 384)]
-    bias_rows = jnp.pad(expand_bias.reshape(hidden // 128, 128), ((0, -(hidden // 128) % 8), (0, 0)))
-    (self_weights, cross_weights, keyval, expand, shrink), biases = gather_shards(shards, bias_rows, chunks, own)
-    bias = biases[:, : hidden // 128].reshape(parts, hidden)
-
+    norms = [first_gain, first_shift, second_gain, second_shift, third_gain, third_shift, expand_bias]
+    norms = jnp.stack(norms + [jnp.zeros_like(expand_bias)])
     counts = image_rows[0]
     ends = jnp.cumsum(counts)
     row_index = plane * rows + jnp.arange(rows, dtype=jnp.int32)
@@ -770,65 +979,61 @@
     slot = jnp.arange(2 * slots, dtype=jnp.int32)
     key_ok = (slot % slots)[None, :] < jnp.repeat(lengths.reshape(pairs, 2), slots, axis=1)
     pair_ok = (key_ok[:, None, :] & ((slot // slots)[:, None] == (slot // slots)[None, :])[None]).astype(f32)
+    patches = jnp.pad(patches, ((0, 0), (0, padded - cells), (0, 0)))
     near = lax.dynamic_slice_in_dim(patches, start, window, 0)
-    near = jnp.pad(near, ((0, 0), (0, padded - cells), (0, 0)))
     image = owner - start
 
     text = tokens.reshape(amount, width)
-    row = lambda vector: vector.reshape(1, width)
-    flat, unit_row, vector = (amount, width), (amount, 128), ((1, width), f32)
+    flat, unit_row = (amount, width), ((amount, 128), f32)
     low_flat, full_flat = (flat, bf16), (flat, f32)
     probs_self, probs_cross = (pairs, tiles_of, 4 * slots, 2 * slots), (rows, tiles_of, 2 * slots, padded)
-    image_part = ((window, padded, width), bf16)
+    image_part, vector = ((window, padded, width), bf16), ((16, width), f32)
+    weights, biases, saved = forward(
+        image,
+        [text, pair_ok, cell_ok, norms],
+        patches,
+        shards,
+        start,
+        window,
+        [low_flat] * 3 + [(probs_self, bf16), low_flat, full_flat, unit_row, low_flat, low_flat]
+        + [image_part, image_part, (probs_cross, bf16), low_flat, full_flat, unit_row, full_flat, low_flat],
+        chunks,
+        own,
+    )
+    self_weights, cross_weights, keyval, expand, shrink = weights
     (
         queries, keys, values, self_probs, self_context, first_unit, first_inverse, first_low, cross_queries, image_keys,
         image_values, cross_probs, cross_context, second_unit, second_inverse, second_value, second_low,
-    ) = on_core(
-        forward_kernel,
-        "forward",
-        [image, text, near, pair_ok, cell_ok, self_weights, cross_weights, keyval]
-        + [row(v) for v in (first_gain, first_shift, second_gain, second_shift)],
-        [low_flat] * 3 + [(probs_self, bf16), low_flat, full_flat, (unit_row, f32), low_flat, low_flat]
-        + [image_part, image_part, (probs_cross, bf16), low_flat, full_flat, (unit_row, f32), full_flat, low_flat],
-        [full_flat] * 3,
-        scalars=1,
-    )
-    joined, expand_grad, shrink_grad, bias_grad, third_gain_grad, third_shift_grad, second_up = on_core(
+    ) = saved
+    joined, expand_grad, shrink_grad, feed_vectors, second_up = on_slots(
         feed_kernel,
         "feed",
-        [second_value, second_low, expand, shrink, bias, row(third_gain), row(third_shift), cotangent.reshape(flat)],
-        [low_flat, (expand.shape, bf16), (shrink.shape, bf16), (bias.shape, f32), vector, vector, full_flat],
-        [((parts,) + flat, bf16)] * 2 + [full_flat, full_flat, (unit_row, f32), low_flat],
+        image,
+        [second_value, second_low, norms, biases, expand, shrink, cotangent.reshape(flat)],
+        [low_flat, (expand.shape, bf16), (shrink.shape, bf16), vector, full_flat],
+        [((parts,) + flat, bf16)] * 2 + [full_flat, full_flat, unit_row, low_flat],
+        parts_in=(4, 5),
+        parts_out=(1, 2),
     )
-    cross_weights_grad, keyval_grad, patch, second_gain_grad, second_shift_grad, first_up = on_core(
+    cross_weights_grad, keyval_grad, patch, cross_vectors, first_up = on_slots(
         cross_back_kernel,
         "cross_back",
-        [image, near, cross_weights, keyval, cross_queries, image_keys, image_values, cross_probs, cross_context, second_up]
-        + [second_unit, second_inverse, row(second_gain), first_low],
+        image,
+        [second_up, second_unit, second_inverse, norms, cross_weights, cross_context, cross_queries, image_values]
+        + [image_keys, cross_probs, first_low, keyval, near],
         [(cross_weights.shape, bf16), (keyval.shape, bf16), ((parts, window, padded, depth // parts), bf16)]
-        + [vector, vector, full_flat],
+        + [vector, full_flat],
         [low_flat, full_flat, full_flat, (image_part[0], f32), (image_part[0], f32), low_flat],
-        scalars=1,
     )
-    self_weights_grad, first_gain_grad, first_shift_grad, text_grad = on_core(
+    self_weights_grad, self_vectors, text_grad = on_slots(
         self_back_kernel,
         "self_back",
-        [text, self_weights, queries, keys, values, self_probs, self_context, first_up, first_unit, first_inverse]
-        + [row(first_gain)],
-        [(self_weights.shape, bf16), vector, vector, full_flat],
+        image,
+        [first_up, first_unit, first_inverse, norms, self_weights, self_context, queries, keys, values, self_probs, text],
+        [(self_weights.shape, bf16), vector, full_flat],
         [low_flat] * 5,
     )
-    vectors = jnp.concatenate(
-        [bias_grad.reshape(-1)]
-        + [
-            grad.reshape(-1)
-            for grad in (
-                first_gain_grad, first_shift_grad, second_gain_grad, second_shift_grad, third_gain_grad, third_shift_grad
-            )
-        ]
-    )
-    entries = vectors.shape[0]
-    vectors = jnp.pad(vectors.reshape(entries // 128, 128), ((0, -(entries // 128) % 8), (0, 0)))
+    vectors = feed_vectors + cross_vectors + self_vectors
     grads = [self_weights_grad, cross_weights_grad, keyval_grad, expand_grad, shrink_grad]
     order = [(4, 0, 768), (3, 0, 768), (1, 0, 384), (2, 0, 384), (0, 0, 768)]
     sums, windows, vectors = reduce_shards(grads, patch, vectors, order, own)
@@ -837,23 +1042,22 @@
         scalars=1,
     )
     self_sum, cross_sum, keyval_sum, expand_sum, shrink_sum = (total.astype(f32) for total in sums)
-    vectors = vectors.reshape(-1)
-    bias_sum = lax.dynamic_slice_in_dim(vectors, plane * hidden, hidden, 0)
-    norms = [vectors[parts * hidden + i * width : parts * hidden + (i + 1) * width] for i in range(6)]
+    bias_sum = lax.dynamic_index_in_dim(vectors, plane, 0, keepdims=False)
+    norms = [vectors[parts + i] for i in range(6)]
     return (
         joined.reshape(tokens.shape),
         text_grad.reshape(tokens.shape),
         patch_grad,
-        jnp.stack([self_sum[c * inner : (c + 1) * inner].T for c in range(3)]),
+        self_sum[: 3 * inner].reshape(3, inner, width).transpose(0, 2, 1),
         self_sum[3 * inner :],
         norms[0],
         norms[1],
         cross_sum[:inner].T,
-        jnp.stack([keyval_sum[:inner].T, keyval_sum[inner:].T]),
+        keyval_sum.reshape(2, inner, depth).transpose(0, 2, 1),
         cross_sum[inner:],
         norms[2],
         norms[3],
-        expand_sum.T,
+        expand_sum,
         bias_sum,
         shrink_sum,
         norms[4],

time: 513 us -> 413 us (0.81); the launches traced: 506 us -> 412 us
  Pallas kernels: 460 us -> 372 us
    pallas_call x5 -> x1, Pallas kernels: 207 us -> 4.28 us  [on_core(): pl.pallas_call(kernel, out_shape=[jax.ShapeDtypeStruct(shape, kind) for s...]
    pallas_call x1 -> x4, Pallas kernels: 90.4 us -> 209 us  [the longest x3 108 us: on_slots(): pl.pallas_call(body, out_shape=[jax.ShapeDtypeStruct(shape, kind) for sha...]
    unnamed x60 -> x16, local copies, waits for them, and re-layouts: 11.3 us -> 9 us
where the time goes in v3:
time: 413 us; the launch traced here: 412 us
  Pallas kernels  372 us (90%)
  local copies, waits for them, and re-layouts  28.6 us (7%)
  other arithmetic  10.4 us (3%)
    pallas_call x1, Pallas kernels, reduce_grads(): pl.pallas_call(functools.partial(reduce_kernel, chunks, count), out_shape...  159 us
    pallas_call x3, Pallas kernels, on_slots(): pl.pallas_call(body, out_shape=[jax.ShapeDtypeStruct(shape, kind) for sha...  108 us
    pallas_call x1, Pallas kernels, gather_forward(): pl.pallas_call(functools.partial(forward_kernel, chunks, [len(pieces) for...  101 us
    unnamed x16, local copies, waits for them, and re-layouts  9 us

profile of v3, /device:TPU:0, one launch (start us, length us, event | category | flops | bytes accessed | tf_op | source)
XLA Modules:
  0.0 412.0 jit_solution(11413939972529424313)
XLA Ops:
  0.7 0.7 dynamic_slice.17
  1.4 0.5 iota_multiply_fusion.starts
  1.9 0.7 stack.24
  2.6 0.7 stack.25
  3.3 0.7 stack.26
  4.0 0.7 stack.27
  4.7 0.7 stack.30
  5.4 0.7 stack.28
  6.1 0.7 stack.29
  6.8 0.6 stack.31.refs_4_.refs_2_.refs_3_
  7.4 0.1 reshape.172
  7.5 0.1 broadcast_in_dim.2
  7.6 0.1 reshape.173
  7.7 0.7 copy.45
  8.4 0.1 reduce
  8.5 0.7 fusion.1
  9.2 0.2 convert_reduce_fusion
  9.4 0.5 broadcast_subtract_fusion.refs_0_.image_ref
  9.9 0.2 compare_reduce_fusion
  10.1 0.8 fusion
  10.9 0.1 broadcast_compare_fusion
  11.0 0.6 pad_convert_fusion.refs_3_
  11.6 0.8 and_convert_fusion.refs_2_
  12.3 5.0 %copy.46 = bf16[16,145,1024]{2,1,0:T(8,128)(2,1)S(1)} copy(bf16[16,145,1024]{2,0,1:T(8,128)(2,1)} %param.23) | data formatting | bytes 9502720 | tf_op args[1]
  17.3 2.4 constant_dynamic-slice_fusion.refs_12_
  19.7 3.2 pad.12.refs_5_
  22.9 100.6 %gather_forward.1 = (bf16[4,768,768]{2,1,0:T(8,128)(2,1)}, bf16[4,384,768]{2,1,0:T(8,128)(2,1)}, bf16[4,384,1024]{2,1,0:T(8,128)(2,1)}, bf16[4,768,768]{2,1,0:T(...) custom-call(s32[16]{0:T(128)} %broadcast_subtract_fusion.refs_0_.ima, ...), custom_call_target="tpu_custom_call" | custom-call | tf_op jit(solution)/shard_map/gather_forward/pallas_call | solution.py:231
  123.5 52.9 %feed.1 = (bf16[640,768]{1,0:T(8,128)(2,1)}, bf16[4,768,768]{2,1,0:T(8,128)(2,1)}, bf16[4,768,768]{2,1,0:T(8,128)(2,1)}, f32[16,768]{1,0:T(8,128)}, f32[640,768]{1,0:T(8,128)}) custom-call(s32[16]{0:T(128)} %broadcast_subtract_fusion.refs_0_.image_ref, f32[640,768]{1,0:T(8,128)} %get-tuple-element.60.refs_0_, bf16[640,768]{1,0:T(8,128)(2,1)} %get-tuple-element.61.refs_1_, ...), custom_call_target="tpu_custom_call" | custom-call | tf_op jit(solution)/shard_map/feed/pallas_call | solution.py:527
  176.5 35.1 %cross_back.1 = (bf16[4,384,768]{2,1,0:T(8,128)(2,1)}, bf16[4,384,1024]{2,1,0:T(8,128)(2,1)}, bf16[4,10,160,256]{3,2,1,0:T(8,128)(2,1)}, f32[16,768]{1,0:T(8,128)}, f32[640,768]{1,0:T(8,128)}) custom-call(s32[16]{0:T(128)} %broadcast_subtract_fusion.refs_0_.image_ref, f32[640,768]{1,0:T(8,128)} %get-tuple-element.66.refs_0_, ...), custom_call_target="tpu_custom_call" | custom-call | tf_op jit(solution)/shard_map/cross_back/pallas_call | solution.py:527
  211.6 0.0 copy-start.5
  211.6 0.0 copy-start.6
  211.6 20.4 %self_back.1 = (bf16[4,768,768]{2,1,0:T(8,128)(2,1)}, f32[16,768]{1,0:T(8,128)}, f32[640,768]{1,0:T(8,128)}) custom-call(s32[16]{0:T(128)} %broadcast_subtract_fusion.refs_0_.image_ref, f32[640,768]{1,0:T(8,128)} %get-tuple-element.77.refs_0_, f32[640,768]{1,0:T(8,128)} %get-tuple-element.78.refs_1_, f32[640,128]{1,0:T(8,128)} %get-tuple-element.79.refs_2_, ...), custom_call_target="tpu_custom_call" | custom-call | tf_op jit(solution)/shard_map/self_back/pallas_call | solution.py:527
  232.0 0.0 copy-done.5
  232.0 0.0 copy-done.6
  232.0 1.4 add_add_fusion.refs_6_
  233.4 158.7 %reduce_grads.1 = (bf16[768,768]{1,0:T(8,128)(2,1)}, bf16[384,768]{1,0:T(8,128)(2,1)}, bf16[384,1024]{1,0:T(8,128)(2,1)}, bf16[768,768]{1,0:T(8,128)(2,1)}, bf16...) custom-call(bf16[4,768,768]{2,1,0:T(8,128)(2,1)} %get-tuple-element.87.refs_0_, ...), custom_call_target="tpu_custom_call" | custom-call | tf_op jit(solution)/shard_map/reduce_grads/pallas_call | solution.py:459
  392.1 4.3 %place.1 = f32[16,145,256]{2,1,0:T(8,128)} custom-call(s32[4]{0:T(128)} %iota_multiply_fusion.starts, bf16[4,10,160,256]{3,2,1,0:T(8,128)(2,1)} %get-tuple-element.96.windows), custom_call_target="tpu_custom_call" | custom-call | tf_op jit(solution)/shard_map/place/pallas_call | solution.py:904
  396.4 0.0 copy-start
  396.4 4.0 copy.47
  400.4 1.5 slice_reduce_fusion
  401.9 0.8 slice.53
  402.7 0.0 copy-start.1
  402.7 0.6 dynamic-slice_reduce_fusion
  403.3 0.0 copy-done
  403.3 0.9 slice.57
  404.2 1.3 slice.56
  405.5 0.0 copy-start.4
  405.5 0.0 copy-done.1
  405.5 0.9 slice.59
  406.4 0.0 copy-start.3
  406.4 0.1 convert_element_type.27
  406.5 0.9 slice_bitcast_fusion
  407.3 0.0 copy-done.4
  407.3 0.0 copy-start.2
  407.3 1.3 convert_bitcast_fusion
  408.6 0.0 copy-done.3
  408.6 1.6 convert_element_type.28
  410.2 0.0 copy-done.2
  410.2 1.6 convert_element_type.29
  (5 shorter events, 0.1 us)
Async XLA Ops:
  211.6 20.4 %copy-start.5 = (f32[16,768]{1,0:T(8,128)S(1)}, f32[16,768]{1,0:T(8,128)}, u32[]{:S(2)}) copy-start(f32[16,768]{1,0:T(8,128)} %get-tuple-element.93) | copy-start | bytes 147460
  211.6 20.4 %copy-start.6 = (f32[16,768]{1,0:T(8,128)S(1)}, f32[16,768]{1,0:T(8,128)}, u32[]{:S(2)}) copy-start(f32[16,768]{1,0:T(8,128)} %get-tuple-element.94) | copy-start | bytes 147460
  396.4 6.9 %copy-start = (bf16[768,768]{1,0:T(8,128)(2,1)S(1)}, bf16[768,768]{1,0:T(8,128)(2,1)}, u32[]{:S(2)}) copy-start(bf16[768,768]{1,0:T(8,128)(2,1)} %get-tuple-element.97) | copy-start | bytes 3538948
  402.7 2.8 copy-start.1
  405.5 1.8 copy-start.4
  406.4 2.3 copy-start.3
  407.3 2.9 copy-start.2
